TPU v7x, 128 devices: a whole 4x4x4 slice. The times are simulated.
128 devices in a mesh: sample: 16 (over z_lo, y, core), head: 8 (over x, z_hi).
Axes of the slice: x: 4, y: 4, z: 4 (z_hi: 2, z_lo: 2; z = z_hi * 2 + z_lo), core: 2. Of those that a mesh axis runs over, the one named last changes fastest.
Arguments:
- queries: bfloat16 [16, 512, 8192], P('sample', None, 'head'), may hold values from -12 to 12
- suffix_keys: bfloat16 [16, 512, 1024], P('sample', None, 'head'), may hold values from -4 to 4
- suffix_values: bfloat16 [16, 512, 1024], P('sample', None, 'head'), may hold values from -16 to 16
- prefix_keys: bfloat16 [4096, 1024], P('sample', 'head'), may hold values from -6 to 6
- prefix_values: bfloat16 [4096, 1024], P('sample', 'head'), may hold values from -16 to 16
- lengths: int32 [16], replicated, may hold values from 1 to 512, as said below
- out_weight: bfloat16 [8192, 5120], P('head', 'sample'), may hold values from -0.0625 to 0.0625
Outputs:
- projected: bfloat16 [16, 512, 5120], P('sample', 'head')
Inputs may be any that keep to these rules, and one draw needn't show every extreme that they name: `lengths`: some sample's length is exactly 512.
All inputs are finite; a program needn't handle non-finite values.
Results may differ from a plain program's by a relative error of at most 0.018.
Values may be sent and summed in bfloat16 or wider, within the bound.
No kernel may reach another device: no remote copies, remote signals or barrier semaphores. Data moves between devices by JAX's collectives and lax.ppermute only.
A program may use at most 128 MiB of HBM per device.

v0:
```python
import functools
import math

import jax
import jax.numpy as jnp
from jax import lax
from jax.experimental import pallas as pl
from jax.experimental.pallas import tpu as pltpu
from jax.sharding import PartitionSpec as P

HD = 128
HEADS = 4
TILE = 256
SCALE = HD ** (-0.5) * math.log2(math.e)
BF = jnp.bfloat16
F32 = jnp.float32
NT = (((1,), (1,)), ((), ()))


def sample_pairs(to):
    place = lambda z, y, c: (z * 4 + y) * 2 + c
    return [
        (place(z, y, c), place(*to(z, y, c)))
        for z in range(2) for y in range(4) for c in range(2)
    ]


def head_pairs(to):
    pairs = []
    for x in range(4):
        for z in range(2):
            tx, tz = to(x, z)
            pairs.append((x * 2 + z, tx * 2 + tz))
    return pairs


CORE = sample_pairs(lambda z, y, c: (z, y, 1 - c))
ZLO = sample_pairs(lambda z, y, c: (1 - z, y, c))
YUP = sample_pairs(lambda z, y, c: (z, (y + 1) % 4, c))
YDOWN = sample_pairs(lambda z, y, c: (z, (y + 3) % 4, c))
YFAR = sample_pairs(lambda z, y, c: (z, (y + 2) % 4, c))
XUP = head_pairs(lambda x, z: ((x + 1) % 4, z))
XDOWN = head_pairs(lambda x, z: ((x + 3) % 4, z))
XFAR = head_pairs(lambda x, z: ((x + 2) % 4, z))
ZHI = head_pairs(lambda x, z: (x, 1 - z))


def over_sample(value, pairs):
    return lax.ppermute(value, "sample", pairs)


def over_head(value, pairs):
    return lax.ppermute(value, "head", pairs)


X, Z_HI, CORE_AT, Y, Z_LO, LENGTH = range(6)


def attend_kernel(counts, samples, first, last, place_ref, q_own_ref, q_got_ref, *refs):
    refs = list(refs)
    suffix_refs = [refs.pop(0) for _ in range(4)] if first else None
    kv_refs = [refs.pop(0) for _ in counts]
    acc_in, stat_in = (None, None) if first else (refs.pop(0), refs.pop(0))
    if last:
        out_ref = refs.pop(0)
    else:
        acc_out, stat_out = refs.pop(0), refs.pop(0)
    keys_ref, values_ref = refs.pop(0), refs.pop(0)
    step, tile = pl.program_id(0), pl.program_id(1)
    sample = samples[0] + step
    rows_total = keys_ref.shape[0]

    @pl.when((step == 0) & (tile == 0))
    def _():
        at = 0
        for kv_ref, count in zip(kv_refs, counts):
            for b in range(count):
                block = kv_ref[b]
                rows = block.shape[0]
                keys_ref[at:at + rows] = block[:, :HD]
                values_ref[at:at + rows, :HD] = block[:, HD:]
                at += rows
        values_ref[:, HD:] = jnp.ones((rows_total, HD), BF)

    length = place_ref[LENGTH + sample]
    live = tile * TILE < length

    def pick(own, got):
        if len(samples) == 1:
            return got if samples[0] else own
        return jnp.where(sample == 0, own, got)

    def fold(state, scores, values):
        top = jnp.max(scores, axis=1, keepdims=True)
        if state is None:
            weights = jnp.exp2((scores - top) * SCALE)
            return top, jnp.dot(weights.astype(BF), values, preferred_element_type=F32)
        old, acc = state
        top = jnp.maximum(old, top)
        weights = jnp.exp2((scores - top) * SCALE)
        part = jnp.dot(weights.astype(BF), values, preferred_element_type=F32)
        return top, acc * jnp.exp2((old - top) * SCALE) + part

    def body(tile_static):
        for h in range(HEADS):
            cols = slice(h * HD, (h + 1) * HD)
            q = pick(q_own_ref[:, cols], q_got_ref[:, cols])
            state = None
            if first:
                row = lax.broadcasted_iota(jnp.int32, (TILE, TILE), 0)
                col = lax.broadcasted_iota(jnp.int32, (TILE, TILE), 1)
                for t in range(tile_static, -1, -1):
                    lines = slice(t * TILE, (t + 1) * TILE)
                    keys, values = (
                        pick(suffix_refs[i][lines], suffix_refs[i + 2][lines]) for i in (0, 1)
                    )
                    scores = lax.dot_general(q, keys, NT, preferred_element_type=F32)
                    if t == tile_static:
                        scores = jnp.where(col <= row, scores, -1e30)
                    values = jnp.concatenate([values, jnp.ones((TILE, HD), BF)], 1)
                    state = fold(state, scores, values)
            at = 0
            size = TILE if first else rows_total
            while at < rows_total:
                scores = lax.dot_general(q, keys_ref[at:at + size], NT, preferred_element_type=F32)
                state = fold(state, scores, values_ref[at:at + size])
                at += size
            top, acc = state
            num, den = acc[:, :HD], acc[:, HD:]
            if not first:
                top = jnp.broadcast_to(top, (TILE, HD))
                old = jnp.broadcast_to(stat_in[:, h:h + 1], (TILE, HD))
                total = jnp.broadcast_to(stat_in[:, HEADS + h:HEADS + h + 1], (TILE, HD))
                new = jnp.maximum(old, top)
                keep, add = jnp.exp2((old - new) * SCALE), jnp.exp2((top - new) * SCALE)
                num = acc_in[:, cols] * keep + num * add
                den = total * keep + den * add
                top = new[:, :1]
            if last:
                row = tile * TILE + lax.broadcasted_iota(jnp.int32, (TILE, HD), 0)
                out_ref[:, cols] = jnp.where(row < length, num / den, 0.0).astype(BF)
            else:
                acc_out[:, cols] = num
                stat_out[:, h:h + 1] = top
                stat_out[:, HEADS + h:HEADS + h + 1] = den[:, :1]

    if first:
        for t in range(2):
            pl.when(live & (tile == t))(functools.partial(body, t))
    else:
        pl.when(live)(functools.partial(body, 0))

    if last:
        @pl.when(jnp.logical_not(live))
        def _():
            out_ref[...] = jnp.zeros_like(out_ref)


def attend(place, q_own, q_got, suffixes, kvs, state, samples, last, name):
    first = state is None
    rows, width = q_got.shape[0], q_got.shape[1] // 2
    counts = [kv.shape[0] for kv in kvs]
    keys_total = sum(kv.shape[0] * kv.shape[1] for kv in kvs)
    tiled = lambda w, base: pl.BlockSpec((None, TILE, w), lambda s, t, p: (base + s, t, 0))
    whole = lambda a: pl.BlockSpec(a.shape, lambda s, t, p: (0,) * a.ndim)
    in_specs = [
        pl.BlockSpec((TILE, width), lambda s, t, p: (t, p[CORE_AT])),
        pl.BlockSpec((TILE, width), lambda s, t, p: (t, p[CORE_AT])),
    ]
    args = [q_own, q_got]
    for array in ([*suffixes] if first else []) + kvs:
        in_specs.append(whole(array))
        args.append(array)
    if not first:
        in_specs += [tiled(width, samples[0]), tiled(HD, samples[0])]
        args += list(state)
    count = len(samples)
    if last:
        out_specs = tiled(width, 0)
        out_shape = jax.ShapeDtypeStruct((count, rows, width), BF)
    else:
        out_specs = [tiled(width, 0), tiled(HD, 0)]
        out_shape = [
            jax.ShapeDtypeStruct((count, rows, width), F32),
            jax.ShapeDtypeStruct((count, rows, HD), F32),
        ]
    keys_seen = keys_total + (rows // 2 if first else 0)
    return pl.pallas_call(
        functools.partial(attend_kernel, counts, samples, first, last),
        grid_spec=pltpu.PrefetchScalarGridSpec(
            num_scalar_prefetch=1,
            grid=(count, rows // TILE),
            in_specs=in_specs,
            out_specs=out_specs,
            scratch_shapes=[
                pltpu.VMEM((keys_total, HD), BF),
                pltpu.VMEM((keys_total, 2 * HD), BF),
            ],
        ),
        out_shape=out_shape,
        name=name,
        cost_estimate=pl.CostEstimate(
            flops=count * rows * HEADS * keys_seen * HD * 32,
            bytes_accessed=4 * count * 2**20,
            transcendentals=count * rows * HEADS * keys_seen,
        ),
        compiler_params=pltpu.CompilerParams(vmem_limit_bytes=48 * 2**20),
    )(place, *args)


OTHER, OWN = False, True
FEATURES = 320


def project_kernel(tiles, count, spans, outs, place_ref, *refs):
    weight_refs = refs[:2 * tiles]
    rows_refs = refs[2 * tiles:2 * tiles + 4 * count]
    add_refs = refs[2 * tiles + 4 * count:-1 - outs]
    out_refs, held_ref = refs[-1 - outs:-1], refs[-1]
    tile = pl.program_id(0)
    own = jnp.concatenate([r[...] for b in range(count) for r in rows_refs[4 * b:4 * b + 2]], axis=0)
    other = jnp.concatenate(
        [r[...] for b in range(count) for r in rows_refs[4 * b + 2:4 * b + 4]], axis=0
    )

    def bring(at):
        held_ref[0] = weight_refs[2 * at][...]
        held_ref[1] = weight_refs[2 * at + 1][...]

    for at in range(tiles):
        pl.when(tile == at)(functools.partial(bring, at))
    acc = lax.dot_general(held_ref[0], own, NT, preferred_element_type=F32)
    acc += lax.dot_general(held_ref[1], other, NT, preferred_element_type=F32)
    for ref, (start, length) in zip(add_refs, spans):
        here = (tile >= start) & (tile < start + length)
        acc += ref[...].astype(F32) if length == tiles else jnp.where(here, ref[...].astype(F32), 0.0)
    lanes = acc.shape[1] // outs
    for k, out_ref in enumerate(out_refs):
        out_ref[...] = acc[:, k * lanes:(k + 1) * lanes].astype(out_ref.dtype)


def project(place, weights, rows, blocks, adds, name, *kinds):
    tiles = len(weights)
    size = FEATURES
    kinds = kinds or (BF,)
    part, depth = rows[0].shape[1:]
    lanes = 2 * part * len(blocks)

    def rows_spec(step, own):
        def index(i, p):
            z = p[Z_HI] if own else 1 - p[Z_HI]
            return (2 * lax.rem(p[X] + step, 4) + z, 0, 0)

        return pl.BlockSpec((None, part, depth), index)

    def add_spec(lane, start, count):
        return pl.BlockSpec(
            (size, lanes), lambda i, p: (jnp.clip(i - start, 0, count - 1), lane)
        )

    in_specs, args = [], []
    for weight, at in weights:
        in_specs.append(pl.BlockSpec((size, depth), lambda i, p, at=at: (at, p[CORE_AT])))
        in_specs.append(pl.BlockSpec((size, depth), lambda i, p, at=at: (at, 1 - p[CORE_AT])))
        args += [weight, weight]
    for block in blocks:
        in_specs += [rows_spec(*block)] * 4
        args += rows
    for array, lane, start, count in adds:
        in_specs.append(add_spec(lane, start, count))
        args.append(array)
    wide = lanes // len(kinds)
    results = pl.pallas_call(
        functools.partial(project_kernel, tiles, len(blocks), [a[2:] for a in adds], len(kinds)),
        grid_spec=pltpu.PrefetchScalarGridSpec(
            num_scalar_prefetch=1,
            grid=(tiles,),
            in_specs=in_specs,
            out_specs=[pl.BlockSpec((size, wide), lambda i, p: (i, 0))] * len(kinds),
            scratch_shapes=[pltpu.VMEM((2, size, depth), BF)],
        ),
        out_shape=[jax.ShapeDtypeStruct((tiles * size, wide), kind) for kind in kinds],
        name=name,
        cost_estimate=pl.CostEstimate(
            flops=4 * tiles * size * lanes * depth,
            bytes_accessed=4 * tiles * size * depth + 2 * tiles * size * lanes,
            transcendentals=0,
        ),
        compiler_params=pltpu.CompilerParams(vmem_limit_bytes=32 * 2**20),
    )(place, *args)
    return results if len(kinds) > 1 else results[0]


def gather_kernel(count, base_ref, *refs):
    out_ref = refs[-1]
    halves, whole = refs[:-1 - count], refs[-1 - count:-1]
    lines = base_ref.shape[0] // 2
    for half in range(2):
        at = slice(half * lines, (half + 1) * lines)
        acc = base_ref[at]
        for ref in halves[half::2]:
            acc += ref[...].astype(F32)
        for ref in whole:
            acc += ref[at].astype(F32)
        out_ref[at] = acc.astype(BF)


def gather(base, lane, halves, whole, name):
    lines = base.shape[0]
    halves = [array for pair in halves for array in pair]
    spec = lambda size, at: pl.BlockSpec((size, 128), lambda i: (0, at))
    return pl.pallas_call(
        functools.partial(gather_kernel, len(whole)),
        grid=(1,),
        in_specs=[spec(lines, lane)] + [spec(lines // 2, lane)] * len(halves)
        + [spec(lines, 0)] * len(whole),
        out_specs=spec(lines, 0),
        out_shape=jax.ShapeDtypeStruct((lines, 128), BF),
        name=name,
        cost_estimate=pl.CostEstimate(
            flops=6 * lines * 128, bytes_accessed=20 * lines * 128, transcendentals=0
        ),
        compiler_params=pltpu.CompilerParams(vmem_limit_bytes=32 * 2**20),
    )(base, *halves, *whole)


def sum_over_head(place, weights, rows, tag, beside=()):
    run = lambda w, blocks, adds, name, *kinds: project(
        place, w, rows, blocks, adds, name + tag, *kinds
    )
    both = lambda step: [(step, OTHER), (step, OWN)]
    n = len(weights) // 2
    top, low = weights[:n], weights[n:]
    via_up = over_head(run(top, both(2), [], "far_top"), XUP)
    via_down = over_head(run(low, both(2), [], "far_low"), XDOWN)
    via_up, via_down, beside = lax.optimization_barrier((via_up, via_down, beside))
    below_low = over_head(run(low, both(1), [], "up_low"), XUP)
    above_top = over_head(run(top, both(3), [], "down_top"), XDOWN)
    below_top = over_head(run(top, both(1), [(via_up, 0, 0, n)], "up_top"), XUP)
    above_low = over_head(run(low, both(3), [(via_down, 0, 0, n)], "down_low"), XDOWN)
    own = run(weights, both(0), [], "own", F32)
    arrived = [(below_top, below_low), (above_top, above_low)]
    from_z = over_head(gather(own, 0, arrived, [], "give" + tag), ZHI)
    return from_z, lambda from_z: gather(own, 1, arrived, [from_z], "sum" + tag), beside


def give_z_first(place, weights, rows, tag):
    return project(place, weights, rows, [(step, OTHER) for step in range(4)], [], "give" + tag)


def sum_z_first(place, weights, rows, got, tag):
    steps = [(step, OWN) for step in range(4)]
    adds = [(got, 0, 0, len(weights))]
    return project(place, weights, rows, steps, adds, "steps" + tag, F32, BF, BF, BF)


EARLY_FROM = ((0, 0), (1, 0), (0, 3), (1, 3), (0, 1), (1, 1))
LATE_FROM = ((0, 2), (1, 2))


def finish_kernel(place_ref, from_ref, own_ref, got_ref, *refs):
    out_ref = refs[-1]
    lane = lax.broadcasted_iota(jnp.int32, (64, 128), 1)
    row = lax.broadcasted_iota(jnp.int32, (64, 128), 0)
    turn = lambda array, at: lax.dot_general(
        jnp.where(lane == row + at, 1.0, 0.0).astype(BF), array, NT, preferred_element_type=F32
    )
    own, got = turn(own_ref[...], 0), turn(got_ref[...], 64)
    first = place_ref[CORE_AT] == 0
    even, odd = jnp.where(first, own, got), jnp.where(first, got, own)
    out_ref[...] = jnp.concatenate([even, odd], axis=1).astype(BF)


def finish(place, own, got, chips, out, name):
    wide = 2 * FEATURES
    offsets = jnp.array([d for chip in chips for d in chip], jnp.int32)

    def to(i, p, f):
        z = lax.rem(f[2 * i] + p[Z_LO], 2)
        return (0, z * 4 + lax.rem(f[2 * i + 1] + p[Y], 4))

    part = pl.BlockSpec((FEATURES, 128), lambda i, p, f: (i, 0))
    return pl.pallas_call(
        finish_kernel,
        grid_spec=pltpu.PrefetchScalarGridSpec(
            num_scalar_prefetch=2,
            grid=(len(chips),),
            in_specs=[part, part] + [pl.BlockSpec(memory_space=pl.ANY)] * len(out),
            out_specs=pl.BlockSpec((64, wide), to),
        ),
        out_shape=jax.ShapeDtypeStruct((64, 8 * wide), BF),
        input_output_aliases={4: 0} if out else {},
        name=name,
        cost_estimate=pl.CostEstimate(
            flops=len(chips) * 2 * 64 * 128 * wide,
            bytes_accessed=len(chips) * wide * 400,
            transcendentals=0,
        ),
        compiler_params=pltpu.CompilerParams(vmem_limit_bytes=32 * 2**20),
    )(place, offsets, own, got, *out)


def per_device(
    queries, suffix_keys, suffix_values, prefix_keys, prefix_values, lengths, out_weight
):
    hold = lax.optimization_barrier
    sample = lax.axis_index("sample")
    head = lax.axis_index("head")
    core = sample % 2
    width = queries.shape[2] // 2
    place = jnp.stack([
        head // 2, head % 2, core, (sample // 2) % 4, sample // 8,
        lengths[sample], lengths[sample + 1 - 2 * core],
    ]).astype(jnp.int32)

    kv = jnp.concatenate([prefix_keys, prefix_values], axis=1)
    kv_z = over_sample(kv, ZLO)
    q_own = queries[0]
    q_got = over_sample(q_own, CORE)
    suffix = [suffix_keys[0], suffix_values[0]]
    suffixes = suffix + [over_sample(a, CORE) for a in suffix]
    kv_core = over_sample(kv, CORE)
    w, kv = hold((out_weight.T, kv))
    w_z = over_sample(w, ZLO)
    near = jnp.stack([kv, kv_z])
    ys = [over_sample(near, to) for to in (YUP, YDOWN, YFAR)]

    run = lambda kvs, state, samples, last, name: attend(
        place, q_own, q_got, suffixes, kvs, state, samples, last, name
    )
    state = run([kv[None], kv_core[None]], None, (0, 1), False, "attend_near")
    ys, state, w_z = hold((ys, state, w_z))
    w_pair = jnp.concatenate([w, w_z], axis=0)
    w_up, w_down = over_sample(w_pair, YUP), over_sample(w_pair, YDOWN)
    rest = [jnp.concatenate([kv_z[None]] + ys, axis=0)]
    rest_core = [over_sample(rest[0], CORE)]
    state = run(rest, state, (0, 1), False, "attend_far")
    own = run(rest_core, state, (0,), True, "attend_own")
    own_core = over_sample(own, CORE)
    state, own = hold((state, own))
    partner = run(rest_core, state, (1,), True, "attend_partner")
    partner_core = over_sample(partner, CORE)
    partner, w_up, w_down = hold((partner, w_up, w_down))
    w_far = over_sample(w_up[:FEATURES], YUP)
    wz_far = over_sample(w_down[FEATURES:], YDOWN)

    rows = [a.reshape(8, 64, width) for a in (own, partner, partner_core, own_core)]
    w_early = [(w_pair, 0), (w_pair, 1), (w_up, 0), (w_up, 1), (w_down, 0), (w_down, 1)]
    w_late = [(w_far, 0), (wz_far, 0)]
    give_late = give_z_first(place, w_late, rows, "_late")
    from_z, finish_early, give_late = sum_over_head(place, w_early, rows, "_early", give_late)
    got = over_head(give_late, ZHI)
    own, up, far, down = sum_z_first(place, w_late, rows, got, "_late")
    arrived = [over_head(far, XFAR), over_head(up, XUP), over_head(down, XDOWN)]
    from_z, arrived = hold((from_z, arrived))
    early = finish_early(from_z)
    late = gather(own, 0, [], arrived, "sum_late")

    out = finish(place, early, over_sample(early, CORE), EARLY_FROM, [], "finish_early")
    out = finish(place, late, over_sample(late, CORE), LATE_FROM, [out], "finish_late")
    return out[None]


def solution(mesh):
    placed = (
        P("sample", None, "head"),
        P("sample", None, "head"),
        P("sample", None, "head"),
        P("sample", "head"),
        P("sample", "head"),
        P(),
        P("head", "sample"),
    )
    return jax.shard_map(
        per_device, mesh=mesh, in_specs=placed, out_specs=P("sample", "head", None), check_vma=False
    )
```

profile of v0, /device:TPU:97, one launch (start us, length us, event | category | flops | bytes accessed | tf_op | source)
XLA Modules:
  0.0 123.5 jit_solution(13512553779638812694)
XLA Ops:
  10.4 1.5 %collective-permute-start.3 = (bf16[2,256,256]{2,1,0:T(8,128)(2,1)S(1)}, bf16[2,256,256]{2,1,0:T(8,128)(2,1)S(1)}, u32[]{:S(2)}, u32[]{:S(2)}) collective-permute-start(bf16[2,256,256]{2,1,0:T(8,128)(2,1)S(1)} %pad_maximum_fusion.1), channel_id=1, source_target_pairs={{0,48},{8,56},{16,0},{24,8},{32,16},{40,24},{48,32},{56,40},{64,11... | collective-permute-start | bytes 786440 | tf_op jit(solution)/shard_map/ppermute | solution.py:49
  11.9 1.6 %collective-permute-start.4 = (bf16[2,256,256]{2,1,0:T(8,128)(2,1)S(1)}, bf16[2,256,256]{2,1,0:T(8,128)(2,1)S(1)}, u32[]{:S(2)}, u32[]{:S(2)}) collective-permute-start(bf16[2,256,256]{2,1,0:T(8,128)(2,1)S(1)} %pad_maximum_fusion.1), channel_id=1, source_target_pairs={{0,32},{8,40},{16,48},{24,56},{32,0},{40,8},{48,16},{56,24},{64,96... | collective-permute-start | bytes 786440 | tf_op jit(solution)/shard_map/ppermute | solution.py:49
  15.3 4.6 %attend_near.1 = (f32[2,512,512]{2,1,0:T(8,128)S(1)}, f32[2,512,128]{2,1,0:T(8,128)S(1)}) custom-call(s32[7]{0:T(128)S(1)} %stack.30.place_ref, bf16[512,1024]{1,0:T(8,128)(2,1)S(1)} %bitcast.108, bf16[512,1024]{1,0:T(8,128)(2,1)S(1)} %collective-permute-done.q_got_ref, bf16[512,128]{1,0:T(8,128)(2,1)S(1)} %bitcast.113, bf16[512,128]{1,0:T(8,128)(2,1)S(1)} %bitcast.115, ...), custom_call_target="tpu_custom_call" | custom-call | flops 12884901888 | bytes 8388608 | tf_op jit(solution)/shard_map/attend_near/pallas_call | solution.py:188
  20.0 4.2 %collective-permute-done.4 = bf16[2,256,256]{2,1,0:T(8,128)(2,1)S(1)} collective-permute-done((bf16[2,256,256]{2,1,0:T(8,128)(2,1)S(1)}, bf16[2,256,256]{2,1,0:T(8,128)(2,1)S(1)}, u32[]{:S(2)}, u32[]{:S(2)}) %collective-permute-start.4) | collective-permute-done | bytes 262176 | tf_op jit(solution)/shard_map/ppermute | solution.py:49
  24.9 2.1 %collective-permute-start.11 = (bf16[640,1024]{1,0:T(8,128)(2,1)S(1)}, bf16[640,1024]{1,0:T(8,128)(2,1)S(1)}, u32[]{:S(2)}, u32[]{:S(2)}) collective-permute-start(bf16[640,1024]{1,0:T(8,128)(2,1)S(1)} %constant_dynamic-update-slice_fusion.2.refs_0_.refs_1_.refs_2_.refs_3_), channel_id=1, source_target_pairs={{0,48},{8,56},{16,0},{24,8},{32,16},{40,24},{48,32},{56,40},{64,11... | collective-permute-start | bytes 3932168 | tf_op jit(solution)/shard_map/ppermute | solution.py:49
  28.0 2.5 %collective-permute-start.9 = (bf16[7,256,256]{2,1,0:T(8,128)(2,1)S(1)}, bf16[7,256,256]{2,1,0:T(8,128)(2,1)S(1)}, u32[]{:S(2)}, u32[]{:S(2)}) collective-permute-start(bf16[7,256,256]{2,1,0:T(8,128)(2,1)S(1)} %pad_maximum_fusion.refs_0_), channel_id=1, source_target_pairs={{0,8},{8,0},{16,24},{24,16},{32,40},{40,32},{48,56},{56,48},{64,72... | collective-permute-start | bytes 2752520 | tf_op jit(solution)/shard_map/ppermute | solution.py:49
  30.5 9.1 %attend_far.1 = (f32[2,512,512]{2,1,0:T(8,128)S(1)}, f32[2,512,128]{2,1,0:T(8,128)S(1)}) custom-call(s32[7]{0:T(128)S(1)} %stack.30.place_ref, bf16[512,1024]{1,0:T(8,128)(2,1)S(1)} %bitcast.109, bf16[512,1024]{1,0:T(8,128)(2,1)S(1)} %collective-permute-done.q_got_ref, bf16[7,256,256]{2,1,0:T(8,128)(2,1)S(1)} %pad_maximum_fusion.refs_0_, ...), custom_call_target="tpu_custom_call" | custom-call | flops 30064771072 | bytes 8388608 | tf_op jit(solution)/shard_map/attend_far/pallas_call | solution.py:188
  39.6 3.8 %attend_own.1 = bf16[1,512,512]{2,1,0:T(8,128)(2,1)S(1)} custom-call(s32[7]{0:T(128)S(1)} %stack.30.place_ref, bf16[512,1024]{1,0:T(8,128)(2,1)S(1)} %bitcast.110, bf16[512,1024]{1,0:T(8,128)(2,1)S(1)} %collective-permute-done.q_got_ref, bf16[7,256,256]{2,1,0:T(8,128)(2,1)S(1)} %collective-permute-done.9.refs_0_, ...), custom_call_target="tpu_custom_call" | custom-call | flops 15032385536 | bytes 4194304 | tf_op jit(solution)/shard_map/attend_own/pallas_call | solution.py:188
  43.4 3.8 %attend_partner.1 = bf16[1,512,512]{2,1,0:T(8,128)(2,1)S(1)} custom-call(s32[7]{0:T(128)S(1)} %stack.30.place_ref, bf16[512,1024]{1,0:T(8,128)(2,1)S(1)} %bitcast.111, bf16[512,1024]{1,0:T(8,128)(2,1)S(1)} %collective-permute-done.q_got_ref, bf16[7,256,256]{2,1,0:T(8,128)(2,1)S(1)} %collective-permute-done.9.refs_0_, ...), custom_call_target="tpu_custom_call" | custom-call | flops 15032385536 | bytes 4194304 | tf_op jit(solution)/shard_map/attend_partner/pallas_call | solution.py:188
  47.8 6.2 %collective-permute-done.10.refs_4_.refs_5_.refs_0_.refs_1_.refs_6_.refs_7_ = bf16[640,1024]{1,0:T(8,128)(2,1)S(1)} collective-permute-done((bf16[640,1024]{1,0:T(8,128)(2,1)S(1)}, bf16[640,1024]{1,0:T(8,128)(2,1)S(1)}, u32[]{:S(2)}, u32[]{:S(2)}) %collective-permute-start.10) | collective-permute-done | bytes 1310752 | tf_op jit(solution)/shard_map/ppermute | solution.py:49
  54.3 2.7 %collective-permute-start.13 = (bf16[320,1024]{1,0:T(8,128)(2,1)S(1)}, bf16[320,1024]{1,0:T(8,128)(2,1)S(1)}, u32[]{:S(2)}, u32[]{:S(2)}) collective-permute-start(bf16[320,1024]{1,0:T(8,128)(2,1)S(1)} %slice.7), channel_id=1, source_target_pairs={{0,48},{8,56},{16,0},{24,8},{32,16},{40,24},{48,32},{56,40},{64,11... | collective-permute-start | bytes 1966088 | tf_op jit(solution)/shard_map/ppermute | solution.py:49
  57.0 2.2 %far_top_early.1 = bf16[960,256]{1,0:T(8,128)(2,1)S(1)} custom-call(s32[7]{0:T(128)S(1)} %stack.30.place_ref, bf16[640,1024]{1,0:T(8,128)(2,1)S(1)} %constant_dynamic-update-slice_fusion.2.refs_0_.refs_1_.refs_2_.refs_3_, bf16[640,1024]{1,0:T(8,128)(2,1)S(1)} %constant_dynamic-update-slice_fusion.2.refs_0_.refs_1_.refs_2_.refs_3_, ...), custom_call_target="tpu_custom_call" | custom-call | flops 503316480 | bytes 2457600 | tf_op jit(solution)/shard_map/far_top_early/pallas_call | solution.py:273
  59.2 2.2 %far_low_early.1 = bf16[960,256]{1,0:T(8,128)(2,1)S(1)} custom-call(s32[7]{0:T(128)S(1)} %stack.30.place_ref, bf16[640,1024]{1,0:T(8,128)(2,1)S(1)} %collective-permute-done.10.refs_4_.refs_5_.refs_0_.refs_1_.refs_6_.refs_7_, bf16[640,1024]{1,0:T(8,128)(2,1)S(1)} %collective-permute-done.10.refs_4_.refs_5_.refs_0_.refs_1_.refs_6_.refs_7_, ...), custom_call_target="tpu_custom_call" | custom-call | flops 503316480 | bytes 2457600 | tf_op jit(solution)/shard_map/far_low_early/pallas_call | solution.py:273
  62.9 1.5 %collective-permute-start.17 = (bf16[960,256]{1,0:T(8,128)(2,1)S(1)}, bf16[960,256]{1,0:T(8,128)(2,1)S(1)}, u32[]{:S(2)}, u32[]{:S(2)}) collective-permute-start(bf16[960,256]{1,0:T(8,128)(2,1)S(1)} %far_low_early.1), channel_id=1, source_target_pairs={{0,6},{1,7},{2,0},{3,1},{4,2},{5,3},{6,4},{7,5},{8,14},{9,15},{10,... | collective-permute-start | bytes 1474568 | tf_op jit(solution)/shard_map/ppermute | solution.py:53
  64.4 2.2 %up_low_early.1 = bf16[960,256]{1,0:T(8,128)(2,1)S(1)} custom-call(s32[7]{0:T(128)S(1)} %stack.30.place_ref, bf16[640,1024]{1,0:T(8,128)(2,1)S(1)} %collective-permute-done.10.refs_4_.refs_5_.refs_0_.refs_1_.refs_6_.refs_7_, bf16[640,1024]{1,0:T(8,128)(2,1)S(1)} %collective-permute-done.10.refs_4_.refs_5_.refs_0_.refs_1_.refs_6_.refs_7_, ...), custom_call_target="tpu_custom_call" | custom-call | flops 503316480 | bytes 2457600 | tf_op jit(solution)/shard_map/up_low_early/pallas_call | solution.py:273
  66.7 2.2 %down_top_early.1 = bf16[960,256]{1,0:T(8,128)(2,1)S(1)} custom-call(s32[7]{0:T(128)S(1)} %stack.30.place_ref, bf16[640,1024]{1,0:T(8,128)(2,1)S(1)} %constant_dynamic-update-slice_fusion.2.refs_0_.refs_1_.refs_2_.refs_3_, bf16[640,1024]{1,0:T(8,128)(2,1)S(1)} %constant_dynamic-update-slice_fusion.2.refs_0_.refs_1_.refs_2_.refs_3_, ...), custom_call_target="tpu_custom_call" | custom-call | flops 503316480 | bytes 2457600 | tf_op jit(solution)/shard_map/down_top_early/pallas_call | solution.py:273
  69.0 2.7 %collective-permute-start.21 = (bf16[960,256]{1,0:T(8,128)(2,1)S(1)}, bf16[960,256]{1,0:T(8,128)(2,1)S(1)}, u32[]{:S(2)}, u32[]{:S(2)}) collective-permute-start(bf16[960,256]{1,0:T(8,128)(2,1)S(1)} %down_top_early.1), channel_id=1, source_target_pairs={{0,6},{1,7},{2,0},{3,1},{4,2},{5,3},{6,4},{7,5},{8,14},{9,15},{10,... | collective-permute-start | bytes 1474568 | tf_op jit(solution)/shard_map/ppermute | solution.py:53
  71.7 2.6 %collective-permute-done.13.refs_2_.refs_3_ = bf16[320,1024]{1,0:T(8,128)(2,1)S(1)} collective-permute-done((bf16[320,1024]{1,0:T(8,128)(2,1)S(1)}, bf16[320,1024]{1,0:T(8,128)(2,1)S(1)}, u32[]{:S(2)}, u32[]{:S(2)}) %collective-permute-start.13) | collective-permute-done | bytes 655392 | tf_op jit(solution)/shard_map/ppermute | solution.py:49
  74.3 2.1 %give_late.1 = bf16[640,512]{1,0:T(8,128)(2,1)S(1)} custom-call(s32[7]{0:T(128)S(1)} %stack.30.place_ref, bf16[320,1024]{1,0:T(8,128)(2,1)S(1)} %collective-permute-done.12.refs_0_.refs_1_, bf16[320,1024]{1,0:T(8,128)(2,1)S(1)} %collective-permute-done.12.refs_0_.refs_1_, bf16[320,1024]{1,0:T(8,128)(2,1)S(1)} %collective-permute-done.13.refs_2_.refs_3_, ...), custom_call_target="tpu_custom_call" | custom-call | flops 671088640 | bytes 1966080 | tf_op jit(solution)/shard_map/give_late/pallas_call | solution.py:273
  76.4 2.2 %up_top_early.1 = bf16[960,256]{1,0:T(8,128)(2,1)S(1)} custom-call(s32[7]{0:T(128)S(1)} %stack.30.place_ref, bf16[640,1024]{1,0:T(8,128)(2,1)S(1)} %constant_dynamic-update-slice_fusion.2.refs_0_.refs_1_.refs_2_.refs_3_, bf16[640,1024]{1,0:T(8,128)(2,1)S(1)} %constant_dynamic-update-slice_fusion.2.refs_0_.refs_1_.refs_2_.refs_3_, ...), custom_call_target="tpu_custom_call" | custom-call | flops 503316480 | bytes 2457600 | tf_op jit(solution)/shard_map/up_top_early/pallas_call | solution.py:273
  79.9 2.2 %down_low_early.1 = bf16[960,256]{1,0:T(8,128)(2,1)S(1)} custom-call(s32[7]{0:T(128)S(1)} %stack.30.place_ref, bf16[640,1024]{1,0:T(8,128)(2,1)S(1)} %collective-permute-done.10.refs_4_.refs_5_.refs_0_.refs_1_.refs_6_.refs_7_, bf16[640,1024]{1,0:T(8,128)(2,1)S(1)} %collective-permute-done.10.refs_4_.refs_5_.refs_0_.refs_1_.refs_6_.refs_7_, ...), custom_call_target="tpu_custom_call" | custom-call | flops 503316480 | bytes 2457600 | tf_op jit(solution)/shard_map/down_low_early/pallas_call | solution.py:273
  82.1 1.5 %collective-permute-start.22 = (bf16[960,256]{1,0:T(8,128)(2,1)S(1)}, bf16[960,256]{1,0:T(8,128)(2,1)S(1)}, u32[]{:S(2)}, u32[]{:S(2)}) collective-permute-start(bf16[960,256]{1,0:T(8,128)(2,1)S(1)} %down_low_early.1), channel_id=1, source_target_pairs={{0,6},{1,7},{2,0},{3,1},{4,2},{5,3},{6,4},{7,5},{8,14},{9,15},{10,... | collective-permute-start | bytes 1474568 | tf_op jit(solution)/shard_map/ppermute | solution.py:53
  83.9 4.2 %own_early.1.base_ref = f32[1920,256]{1,0:T(8,128)S(1)} custom-call(s32[7]{0:T(128)S(1)} %stack.30.place_ref, bf16[640,1024]{1,0:T(8,128)(2,1)S(1)} %constant_dynamic-update-slice_fusion.2.refs_0_.refs_1_.refs_2_.refs_3_, bf16[640,1024]{1,0:T(8,128)(2,1)S(1)} %constant_dynamic-update-slice_fusion.2.refs_0_.refs_1_.refs_2_.refs_3_, ...), custom_call_target="tpu_custom_call" | custom-call | flops 1006632960 | bytes 4915200 | tf_op jit(solution)/shard_map/own_early/pallas_call | solution.py:273
  88.1 5.4 %collective-permute-done.19.refs_0_ = bf16[960,256]{1,0:T(8,128)(2,1)S(1)} collective-permute-done((bf16[960,256]{1,0:T(8,128)(2,1)S(1)}, bf16[960,256]{1,0:T(8,128)(2,1)S(1)}, u32[]{:S(2)}, u32[]{:S(2)}) %collective-permute-start.19) | collective-permute-done | bytes 491552 | tf_op jit(solution)/shard_map/ppermute | solution.py:53
  96.7 2.1 %steps_late.1 = (f32[640,128]{1,0:T(8,128)S(1)}, bf16[640,128]{1,0:T(8,128)(2,1)S(1)}, bf16[640,128]{1,0:T(8,128)(2,1)S(1)}, bf16[640,128]{1,0:T(8,128)(2,1)S(1)}) custom-call(s32[7]{0:T(128)S(1)} %stack.30.place_ref, bf16[320,1024]{1,0:T(8,128)(2,1)S(1)} %collective-permute-done.12.refs_0_.refs_1_, ...), custom_call_target="tpu_custom_call" | custom-call | flops 671088640 | bytes 1966080 | tf_op jit(solution)/shard_map/steps_late/pallas_call | solution.py:273
  98.7 1.9 %collective-permute-start.24 = (bf16[640,128]{1,0:T(8,128)(2,1)S(1)}, bf16[640,128]{1,0:T(8,128)(2,1)S(1)}, u32[]{:S(2)}, u32[]{:S(2)}) collective-permute-start(bf16[640,128]{1,0:T(8,128)(2,1)S(1)} %get-tuple-element.56), channel_id=1, source_target_pairs={{0,4},{1,5},{2,6},{3,7},{4,0},{5,1},{6,2},{7,3},{8,12},{9,13},{10,... | collective-permute-start | bytes 491528 | tf_op jit(solution)/shard_map/ppermute | solution.py:53
  101.3 2.1 %collective-permute-start.26 = (bf16[640,128]{1,0:T(8,128)(2,1)S(1)}, bf16[640,128]{1,0:T(8,128)(2,1)S(1)}, u32[]{:S(2)}, u32[]{:S(2)}) collective-permute-start(bf16[640,128]{1,0:T(8,128)(2,1)S(1)} %get-tuple-element.58), channel_id=1, source_target_pairs={{0,6},{1,7},{2,0},{3,1},{4,2},{5,3},{6,4},{7,5},{8,14},{9,15},{10,... | collective-permute-start | bytes 491528 | tf_op jit(solution)/shard_map/ppermute | solution.py:53
  104.8 1.8 %collective-permute-done.25.refs_1_ = bf16[640,128]{1,0:T(8,128)(2,1)S(1)} collective-permute-done((bf16[640,128]{1,0:T(8,128)(2,1)S(1)}, bf16[640,128]{1,0:T(8,128)(2,1)S(1)}, u32[]{:S(2)}, u32[]{:S(2)}) %collective-permute-start.25) | collective-permute-done | bytes 163872 | tf_op jit(solution)/shard_map/ppermute | solution.py:53
  106.5 2.8 %collective-permute-done.23.refs_4_ = bf16[1920,128]{1,0:T(8,128)(2,1)S(1)} collective-permute-done((bf16[1920,128]{1,0:T(8,128)(2,1)S(1)}, bf16[1920,128]{1,0:T(8,128)(2,1)S(1)}, u32[]{:S(2)}, u32[]{:S(2)}) %collective-permute-start.23) | collective-permute-done | bytes 491552 | tf_op jit(solution)/shard_map/ppermute | solution.py:53
  109.9 6.8 %collective-permute-start.28 = (bf16[1920,128]{1,0:T(8,128)(2,1)S(1)}, bf16[1920,128]{1,0:T(8,128)(2,1)S(1)}, u32[]{:S(2)}, u32[]{:S(2)}) collective-permute-start(bf16[1920,128]{1,0:T(8,128)(2,1)S(1)} %sum_early.1.own_ref), channel_id=1, source_target_pairs={{0,8},{8,0},{16,24},{24,16},{32,40},{40,32},{48,56},{56,48},{64,72... | collective-permute-start | bytes 1474568 | tf_op jit(solution)/shard_map/ppermute | solution.py:49
  118.2 3.5 %finish_early.1.refs_0_ = bf16[64,5120]{1,0:T(8,128)(2,1)} custom-call(s32[7]{0:T(128)S(1)} %stack.30.place_ref, s32[12]{0:T(128)S(1)} %copy-done.1, bf16[1920,128]{1,0:T(8,128)(2,1)S(1)} %sum_early.1.own_ref, bf16[1920,128]{1,0:T(8,128)(2,1)S(1)} %collective-permute-done.28.got_ref), custom_call_target="tpu_custom_call" | custom-call | flops 62914560 | bytes 1536000 | tf_op jit(solution)/shard_map/finish_early/pallas_call | solution.py:383
  121.8 1.8 %finish_late.1 = bf16[64,5120]{1,0:T(8,128)(2,1)} custom-call(s32[7]{0:T(128)S(1)} %stack.30.place_ref, s32[4]{0:T(128)S(1)} %copy-done, bf16[640,128]{1,0:T(8,128)(2,1)S(1)} %sum_late.1.own_ref, bf16[640,128]{1,0:T(8,128)(2,1)S(1)} %collective-permute-done.27.got_ref, bf16[64,5120]{1,0:T(8,128)(2,1)} %finish_early.1.refs_0_), custom_call_target="tpu_custom_call", output_to_operand_aliasing={{}: (4, {})} | custom-call | flops 20971520 | bytes 512000 | tf_op jit(solution)/shard_map/finish_late/pallas_call | solution.py:383
  (68 shorter events, 25.1 us)
Async XLA Ops:
  0.0 13.5 %copy-start.2 = (bf16[1,512,1024]{2,1,0:T(8,128)(2,1)S(1)}, bf16[1,512,1024]{2,1,0:T(8,128)(2,1)}, u32[]{:S(2)}) copy-start(bf16[1,512,1024]{2,1,0:T(8,128)(2,1)} %param.9) | copy-start | bytes 3145732
  0.0 13.5 %collective-permute-start = (bf16[512,1024]{1,0:T(8,128)(2,1)}, bf16[512,1024]{1,0:T(8,128)(2,1)S(1)}, u32[]{:S(2)}, u32[]{:S(2)}) collective-permute-start(bf16[512,1024]{1,0:T(8,128)(2,1)} %bitcast.107), channel_id=1, source_target_pairs={{0,8},{8,0},{16,24},{24,16},{32,40},{40,32},{48,56},{56,48},{64,72... | collective-permute-start | bytes 3145736 | tf_op jit(solution)/shard_map/ppermute | solution.py:49
  2.4 5.2 %collective-permute-start.1 = (bf16[256,256]{1,0:T(8,128)(2,1)S(1)}, bf16[256,256]{1,0:T(8,128)(2,1)}, u32[]{:S(2)}, u32[]{:S(2)}) collective-permute-start(bf16[256,256]{1,0:T(8,128)(2,1)S(1)} %constant_dynamic-update-slice_fusion), channel_id=1, source_target_pairs={{0,64},{8,72},{16,80},{24,88},{32,96},{40,104},{48,112},{56,120},{... | collective-permute-start | bytes 393224 | tf_op jit(solution)/shard_map/ppermute | solution.py:49
  2.6 9.3 %collective-permute-start.7 = (bf16[256,256]{1,0:T(8,128)(2,1)S(1)}, bf16[256,256]{1,0:T(8,128)(2,1)}, u32[]{:S(2)}, u32[]{:S(2)}) collective-permute-start(bf16[256,256]{1,0:T(8,128)(2,1)S(1)} %constant_dynamic-update-slice_fusion), channel_id=1, source_target_pairs={{0,8},{8,0},{16,24},{24,16},{32,40},{40,32},{48,56},{56,48},{64,72... | collective-permute-start | bytes 393224 | tf_op jit(solution)/shard_map/ppermute | solution.py:49
  3.0 6.0 %collective-permute-start.5 = (bf16[512,128]{1,0:T(8,128)(2,1)}, bf16[512,128]{1,0:T(8,128)(2,1)}, u32[]{:S(2)}, u32[]{:S(2)}) collective-permute-start(bf16[512,128]{1,0:T(8,128)(2,1)} %bitcast.112), channel_id=1, source_target_pairs={{0,8},{8,0},{16,24},{24,16},{32,40},{40,32},{48,56},{56,48},{64,72... | collective-permute-start | bytes 393224 | tf_op jit(solution)/shard_map/ppermute | solution.py:49
  3.1 7.3 %collective-permute-start.6 = (bf16[512,128]{1,0:T(8,128)(2,1)}, bf16[512,128]{1,0:T(8,128)(2,1)}, u32[]{:S(2)}, u32[]{:S(2)}) collective-permute-start(bf16[512,128]{1,0:T(8,128)(2,1)} %bitcast.114), channel_id=1, source_target_pairs={{0,8},{8,0},{16,24},{24,16},{32,40},{40,32},{48,56},{56,48},{64,72... | collective-permute-start | bytes 393224 | tf_op jit(solution)/shard_map/ppermute | solution.py:49
  7.6 16.5 %collective-permute-start.8 = (bf16[320,1024]{1,0:T(8,128)(2,1)}, bf16[320,1024]{1,0:T(8,128)(2,1)S(1)}, u32[]{:S(2)}, u32[]{:S(2)}) collective-permute-start(bf16[320,1024]{1,0:T(8,128)(2,1)} %bitcast.117), channel_id=1, source_target_pairs={{0,64},{8,72},{16,80},{24,88},{32,96},{40,104},{48,112},{56,120},{... | collective-permute-start | bytes 1966088 | tf_op jit(solution)/shard_map/ppermute | solution.py:49
  9.0 10.9 %collective-permute-start.2 = (bf16[2,256,256]{2,1,0:T(8,128)(2,1)S(1)}, bf16[2,256,256]{2,1,0:T(8,128)(2,1)S(1)}, u32[]{:S(2)}, u32[]{:S(2)}) collective-permute-start(bf16[2,256,256]{2,1,0:T(8,128)(2,1)S(1)} %pad_maximum_fusion.1), channel_id=1, source_target_pairs={{0,16},{8,24},{16,32},{24,40},{32,48},{40,56},{48,0},{56,8},{64,80... | collective-permute-start | bytes 786440 | tf_op jit(solution)/shard_map/ppermute | solution.py:49
  10.4 9.6 %collective-permute-start.3 = (bf16[2,256,256]{2,1,0:T(8,128)(2,1)S(1)}, bf16[2,256,256]{2,1,0:T(8,128)(2,1)S(1)}, u32[]{:S(2)}, u32[]{:S(2)}) collective-permute-start(bf16[2,256,256]{2,1,0:T(8,128)(2,1)S(1)} %pad_maximum_fusion.1), channel_id=1, source_target_pairs={{0,48},{8,56},{16,0},{24,8},{32,16},{40,24},{48,32},{56,40},{64,11... | collective-permute-start | bytes 786440 | tf_op jit(solution)/shard_map/ppermute | solution.py:49
  11.9 12.2 %collective-permute-start.4 = (bf16[2,256,256]{2,1,0:T(8,128)(2,1)S(1)}, bf16[2,256,256]{2,1,0:T(8,128)(2,1)S(1)}, u32[]{:S(2)}, u32[]{:S(2)}) collective-permute-start(bf16[2,256,256]{2,1,0:T(8,128)(2,1)S(1)} %pad_maximum_fusion.1), channel_id=1, source_target_pairs={{0,32},{8,40},{16,48},{24,56},{32,0},{40,8},{48,16},{56,24},{64,96... | collective-permute-start | bytes 786440 | tf_op jit(solution)/shard_map/ppermute | solution.py:49
  20.0 8.0 %copy-start.5 = (f32[2,512,512]{2,1,0:T(8,128)}, f32[2,512,512]{2,1,0:T(8,128)S(1)}, u32[]{:S(2)}) copy-start(f32[2,512,512]{2,1,0:T(8,128)S(1)} %get-tuple-element.41.refs_1_) | copy-start | bytes 6291460
  24.2 29.8 %collective-permute-start.10 = (bf16[640,1024]{1,0:T(8,128)(2,1)S(1)}, bf16[640,1024]{1,0:T(8,128)(2,1)S(1)}, u32[]{:S(2)}, u32[]{:S(2)}) collective-permute-start(bf16[640,1024]{1,0:T(8,128)(2,1)S(1)} %constant_dynamic-update-slice_fusion.2.refs_0_.refs_1_.refs_2_.refs_3_), channel_id=1, source_target_pairs={{0,16},{8,24},{16,32},{24,40},{32,48},{40,56},{48,0},{56,8},{64,80... | collective-permute-start | bytes 3932168 | tf_op jit(solution)/shard_map/ppermute | solution.py:49
  24.9 29.2 %collective-permute-start.11 = (bf16[640,1024]{1,0:T(8,128)(2,1)S(1)}, bf16[640,1024]{1,0:T(8,128)(2,1)S(1)}, u32[]{:S(2)}, u32[]{:S(2)}) collective-permute-start(bf16[640,1024]{1,0:T(8,128)(2,1)S(1)} %constant_dynamic-update-slice_fusion.2.refs_0_.refs_1_.refs_2_.refs_3_), channel_id=1, source_target_pairs={{0,48},{8,56},{16,0},{24,8},{32,16},{40,24},{48,32},{56,40},{64,11... | collective-permute-start | bytes 3932168 | tf_op jit(solution)/shard_map/ppermute | solution.py:49
  28.0 11.6 %collective-permute-start.9 = (bf16[7,256,256]{2,1,0:T(8,128)(2,1)S(1)}, bf16[7,256,256]{2,1,0:T(8,128)(2,1)S(1)}, u32[]{:S(2)}, u32[]{:S(2)}) collective-permute-start(bf16[7,256,256]{2,1,0:T(8,128)(2,1)S(1)} %pad_maximum_fusion.refs_0_), channel_id=1, source_target_pairs={{0,8},{8,0},{16,24},{24,16},{32,40},{40,32},{48,56},{56,48},{64,72... | collective-permute-start | bytes 2752520 | tf_op jit(solution)/shard_map/ppermute | solution.py:49
  47.2 9.7 %collective-permute-start.14 = (bf16[1,512,512]{2,1,0:T(8,128)(2,1)S(1)}, bf16[1,512,512]{2,1,0:T(8,128)(2,1)S(1)}, u32[]{:S(2)}, u32[]{:S(2)}) collective-permute-start(bf16[1,512,512]{2,1,0:T(8,128)(2,1)S(1)} %attend_partner.1), channel_id=1, source_target_pairs={{0,8},{8,0},{16,24},{24,16},{32,40},{40,32},{48,56},{56,48},{64,72... | collective-permute-start | bytes 1572872 | tf_op jit(solution)/shard_map/ppermute | solution.py:49
  47.3 9.6 %collective-permute-start.15 = (bf16[1,512,512]{2,1,0:T(8,128)(2,1)S(1)}, bf16[1,512,512]{2,1,0:T(8,128)(2,1)S(1)}, u32[]{:S(2)}, u32[]{:S(2)}) collective-permute-start(bf16[1,512,512]{2,1,0:T(8,128)(2,1)S(1)} %attend_own.1), channel_id=1, source_target_pairs={{0,8},{8,0},{16,24},{24,16},{32,40},{40,32},{48,56},{56,48},{64,72... | collective-permute-start | bytes 1572872 | tf_op jit(solution)/shard_map/ppermute | solution.py:49
  54.1 14.9 %collective-permute-start.12 = (bf16[320,1024]{1,0:T(8,128)(2,1)S(1)}, bf16[320,1024]{1,0:T(8,128)(2,1)S(1)}, u32[]{:S(2)}, u32[]{:S(2)}) collective-permute-start(bf16[320,1024]{1,0:T(8,128)(2,1)S(1)} %slice.6), channel_id=1, source_target_pairs={{0,16},{8,24},{16,32},{24,40},{32,48},{40,56},{48,0},{56,8},{64,80... | collective-permute-start | bytes 1966088 | tf_op jit(solution)/shard_map/ppermute | solution.py:49
  54.3 20.0 %collective-permute-start.13 = (bf16[320,1024]{1,0:T(8,128)(2,1)S(1)}, bf16[320,1024]{1,0:T(8,128)(2,1)S(1)}, u32[]{:S(2)}, u32[]{:S(2)}) collective-permute-start(bf16[320,1024]{1,0:T(8,128)(2,1)S(1)} %slice.7), channel_id=1, source_target_pairs={{0,48},{8,56},{16,0},{24,8},{32,16},{40,24},{48,32},{56,40},{64,11... | collective-permute-start | bytes 1966088 | tf_op jit(solution)/shard_map/ppermute | solution.py:49
  61.4 14.9 %collective-permute-start.16 = (bf16[960,256]{1,0:T(8,128)(2,1)S(1)}, bf16[960,256]{1,0:T(8,128)(2,1)S(1)}, u32[]{:S(2)}, u32[]{:S(2)}) collective-permute-start(bf16[960,256]{1,0:T(8,128)(2,1)S(1)} %far_top_early.1), channel_id=1, source_target_pairs={{0,2},{1,3},{2,4},{3,5},{4,6},{5,7},{6,0},{7,1},{8,10},{9,11},{10,... | collective-permute-start | bytes 1474568 | tf_op jit(solution)/shard_map/ppermute | solution.py:53
  62.9 13.5 %collective-permute-start.17 = (bf16[960,256]{1,0:T(8,128)(2,1)S(1)}, bf16[960,256]{1,0:T(8,128)(2,1)S(1)}, u32[]{:S(2)}, u32[]{:S(2)}) collective-permute-start(bf16[960,256]{1,0:T(8,128)(2,1)S(1)} %far_low_early.1), channel_id=1, source_target_pairs={{0,6},{1,7},{2,0},{3,1},{4,2},{5,3},{6,4},{7,5},{8,14},{9,15},{10,... | collective-permute-start | bytes 1474568 | tf_op jit(solution)/shard_map/ppermute | solution.py:53
  66.6 21.5 %collective-permute-start.20 = (bf16[960,256]{1,0:T(8,128)(2,1)S(1)}, bf16[960,256]{1,0:T(8,128)(2,1)S(1)}, u32[]{:S(2)}, u32[]{:S(2)}) collective-permute-start(bf16[960,256]{1,0:T(8,128)(2,1)S(1)} %up_low_early.1), channel_id=1, source_target_pairs={{0,2},{1,3},{2,4},{3,5},{4,6},{5,7},{6,0},{7,1},{8,10},{9,11},{10,... | collective-permute-start | bytes 1474568 | tf_op jit(solution)/shard_map/ppermute | solution.py:53
  69.0 19.1 %collective-permute-start.21 = (bf16[960,256]{1,0:T(8,128)(2,1)S(1)}, bf16[960,256]{1,0:T(8,128)(2,1)S(1)}, u32[]{:S(2)}, u32[]{:S(2)}) collective-permute-start(bf16[960,256]{1,0:T(8,128)(2,1)S(1)} %down_top_early.1), channel_id=1, source_target_pairs={{0,6},{1,7},{2,0},{3,1},{4,2},{5,3},{6,4},{7,5},{8,14},{9,15},{10,... | collective-permute-start | bytes 1474568 | tf_op jit(solution)/shard_map/ppermute | solution.py:53
  78.6 14.9 %collective-permute-start.19 = (bf16[960,256]{1,0:T(8,128)(2,1)S(1)}, bf16[960,256]{1,0:T(8,128)(2,1)S(1)}, u32[]{:S(2)}, u32[]{:S(2)}) collective-permute-start(bf16[960,256]{1,0:T(8,128)(2,1)S(1)} %up_top_early.1), channel_id=1, source_target_pairs={{0,2},{1,3},{2,4},{3,5},{4,6},{5,7},{6,0},{7,1},{8,10},{9,11},{10,... | collective-permute-start | bytes 1474568 | tf_op jit(solution)/shard_map/ppermute | solution.py:53
  82.1 11.9 %collective-permute-start.22 = (bf16[960,256]{1,0:T(8,128)(2,1)S(1)}, bf16[960,256]{1,0:T(8,128)(2,1)S(1)}, u32[]{:S(2)}, u32[]{:S(2)}) collective-permute-start(bf16[960,256]{1,0:T(8,128)(2,1)S(1)} %down_low_early.1), channel_id=1, source_target_pairs={{0,6},{1,7},{2,0},{3,1},{4,2},{5,3},{6,4},{7,5},{8,14},{9,15},{10,... | collective-permute-start | bytes 1474568 | tf_op jit(solution)/shard_map/ppermute | solution.py:53
  83.7 13.0 %collective-permute-start.18 = (bf16[640,512]{1,0:T(8,128)(2,1)S(1)}, bf16[640,512]{1,0:T(8,128)(2,1)S(1)}, u32[]{:S(2)}, u32[]{:S(2)}) collective-permute-start(bf16[640,512]{1,0:T(8,128)(2,1)S(1)} %give_late.1), channel_id=1, source_target_pairs={{0,1},{1,0},{2,3},{3,2},{4,5},{5,4},{6,7},{7,6},{8,9},{9,8},{10,11... | collective-permute-start | bytes 1966088 | tf_op jit(solution)/shard_map/ppermute | solution.py:53
  94.5 14.9 %collective-permute-start.23 = (bf16[1920,128]{1,0:T(8,128)(2,1)S(1)}, bf16[1920,128]{1,0:T(8,128)(2,1)S(1)}, u32[]{:S(2)}, u32[]{:S(2)}) collective-permute-start(bf16[1920,128]{1,0:T(8,128)(2,1)S(1)} %give_early.1), channel_id=1, source_target_pairs={{0,1},{1,0},{2,3},{3,2},{4,5},{5,4},{6,7},{7,6},{8,9},{9,8},{10,11... | collective-permute-start | bytes 1474568 | tf_op jit(solution)/shard_map/ppermute | solution.py:53
  98.7 6.0 %collective-permute-start.24 = (bf16[640,128]{1,0:T(8,128)(2,1)S(1)}, bf16[640,128]{1,0:T(8,128)(2,1)S(1)}, u32[]{:S(2)}, u32[]{:S(2)}) collective-permute-start(bf16[640,128]{1,0:T(8,128)(2,1)S(1)} %get-tuple-element.56), channel_id=1, source_target_pairs={{0,4},{1,5},{2,6},{3,7},{4,0},{5,1},{6,2},{7,3},{8,12},{9,13},{10,... | collective-permute-start | bytes 491528 | tf_op jit(solution)/shard_map/ppermute | solution.py:53
  100.6 5.9 %collective-permute-start.25 = (bf16[640,128]{1,0:T(8,128)(2,1)S(1)}, bf16[640,128]{1,0:T(8,128)(2,1)S(1)}, u32[]{:S(2)}, u32[]{:S(2)}) collective-permute-start(bf16[640,128]{1,0:T(8,128)(2,1)S(1)} %get-tuple-element.57), channel_id=1, source_target_pairs={{0,2},{1,3},{2,4},{3,5},{4,6},{5,7},{6,0},{7,1},{8,10},{9,11},{10,... | collective-permute-start | bytes 491528 | tf_op jit(solution)/shard_map/ppermute | solution.py:53
  101.2 17.0 %copy-start.1 = (s32[12]{0:T(128)S(1)}, s32[12]{0:T(128)}, u32[]{:S(2)}) copy-start(s32[12]{0:T(128)} %constant.72.clone.from_ref) | copy-start | bytes 148
  101.3 5.3 %collective-permute-start.26 = (bf16[640,128]{1,0:T(8,128)(2,1)S(1)}, bf16[640,128]{1,0:T(8,128)(2,1)S(1)}, u32[]{:S(2)}, u32[]{:S(2)}) collective-permute-start(bf16[640,128]{1,0:T(8,128)(2,1)S(1)} %get-tuple-element.58), channel_id=1, source_target_pairs={{0,6},{1,7},{2,0},{3,1},{4,2},{5,3},{6,4},{7,5},{8,14},{9,15},{10,... | collective-permute-start | bytes 491528 | tf_op jit(solution)/shard_map/ppermute | solution.py:53
  109.9 8.3 %collective-permute-start.28 = (bf16[1920,128]{1,0:T(8,128)(2,1)S(1)}, bf16[1920,128]{1,0:T(8,128)(2,1)S(1)}, u32[]{:S(2)}, u32[]{:S(2)}) collective-permute-start(bf16[1920,128]{1,0:T(8,128)(2,1)S(1)} %sum_early.1.own_ref), channel_id=1, source_target_pairs={{0,8},{8,0},{16,24},{24,16},{32,40},{40,32},{48,56},{56,48},{64,72... | collective-permute-start | bytes 1474568 | tf_op jit(solution)/shard_map/ppermute | solution.py:49
  116.8 5.0 %collective-permute-start.27 = (bf16[640,128]{1,0:T(8,128)(2,1)S(1)}, bf16[640,128]{1,0:T(8,128)(2,1)S(1)}, u32[]{:S(2)}, u32[]{:S(2)}) collective-permute-start(bf16[640,128]{1,0:T(8,128)(2,1)S(1)} %sum_late.1.own_ref), channel_id=1, source_target_pairs={{0,8},{8,0},{16,24},{24,16},{32,40},{40,32},{48,56},{56,48},{64,72... | collective-permute-start | bytes 491528 | tf_op jit(solution)/shard_map/ppermute | solution.py:49
  (4 other events, 11.5 us)
where the time goes:
time: 125 us; the launch traced here: 124 us
  Pallas kernels  49.2 us (39%)
  starting transfers between devices  36.5 us (29%)
  waiting for transfers between devices  28.7 us (23%)
  local copies, waits for them, and re-layouts  6.79 us (5%)
  other arithmetic  1.94 us (2%)
    ppermute x18, starting transfers between devices, over_sample(): return lax.ppermute(value, 'sample', pairs)  22.3 us
    pallas_call x9, Pallas kernels, project(): pl.pallas_call(functools.partial(project_kernel, tiles, len(blocks), [a[2...  21.6 us
    pallas_call x4, Pallas kernels, attend(): pl.pallas_call(functools.partial(attend_kernel, counts, samples, first, l...  21.3 us
    ppermute x18, waiting for transfers between devices, over_sample(): return lax.ppermute(value, 'sample', pairs)  15.4 us
    ppermute x11, starting transfers between devices, over_head(): return lax.ppermute(value, 'head', pairs)  14.2 us
    ppermute x11, waiting for transfers between devices, over_head(): return lax.ppermute(value, 'head', pairs)  13.3 us
    pallas_call x2, Pallas kernels, finish(): pl.pallas_call(finish_kernel, grid_spec=pltpu.PrefetchScalarGridSpec(num_...  5.3 us
    unnamed x16, local copies, waits for them, and re-layouts  3.81 us
  transfers between devices with their start and end apart: 29, of which 11 were waited for; matrix products, arithmetic and copies ran while one was open for 6% of the time, Pallas kernels for 38%

commit v1 on v0

--- a/solution.py
+++ b/solution.py
@@ -358,46 +358,38 @@
 LATE_FROM = ((0, 2), (1, 2))
 
 
-def finish_kernel(place_ref, from_ref, own_ref, got_ref, *refs):
-    out_ref = refs[-1]
-    lane = lax.broadcasted_iota(jnp.int32, (64, 128), 1)
-    row = lax.broadcasted_iota(jnp.int32, (64, 128), 0)
-    turn = lambda array, at: lax.dot_general(
-        jnp.where(lane == row + at, 1.0, 0.0).astype(BF), array, NT, preferred_element_type=F32
-    )
-    own, got = turn(own_ref[...], 0), turn(got_ref[...], 64)
+def finish_kernel(place_ref, own_early_ref, own_late_ref, got_early_ref, got_late_ref, out_ref):
     first = place_ref[CORE_AT] == 0
-    even, odd = jnp.where(first, own, got), jnp.where(first, got, own)
-    out_ref[...] = jnp.concatenate([even, odd], axis=1).astype(BF)
-
-
-def finish(place, own, got, chips, out, name):
     wide = 2 * FEATURES
-    offsets = jnp.array([d for chip in chips for d in chip], jnp.int32)
-
-    def to(i, p, f):
-        z = lax.rem(f[2 * i] + p[Z_LO], 2)
-        return (0, z * 4 + lax.rem(f[2 * i + 1] + p[Y], 4))
-
-    part = pl.BlockSpec((FEATURES, 128), lambda i, p, f: (i, 0))
+    for own_ref, got_ref, chips in (
+        (own_early_ref, got_early_ref, EARLY_FROM), (own_late_ref, got_late_ref, LATE_FROM)
+    ):
+        for at, (dz, dy) in enumerate(chips):
+            lines = slice(at * FEATURES, (at + 1) * FEATURES)
+            own = jnp.transpose(own_ref[lines].astype(F32))[:64]
+            got = jnp.transpose(got_ref[lines].astype(F32))[64:]
+            even, odd = jnp.where(first, own, got), jnp.where(first, got, own)
+            z = lax.rem(place_ref[Z_LO] + dz, 2)
+            to = (z * 4 + lax.rem(place_ref[Y] + dy, 4)) * wide
+            columns = pl.ds(pl.multiple_of(to, 128), wide)
+            out_ref[:, columns] = jnp.concatenate([even, odd], axis=1).astype(BF)
+
+
+def finish(place, own, got):
+    whole = [pl.BlockSpec(a.shape, lambda i, p: (0, 0)) for a in own + got]
+    columns = 2 * FEATURES * (len(EARLY_FROM) + len(LATE_FROM))
     return pl.pallas_call(
         finish_kernel,
         grid_spec=pltpu.PrefetchScalarGridSpec(
-            num_scalar_prefetch=2,
-            grid=(len(chips),),
-            in_specs=[part, part] + [pl.BlockSpec(memory_space=pl.ANY)] * len(out),
-            out_specs=pl.BlockSpec((64, wide), to),
-        ),
-        out_shape=jax.ShapeDtypeStruct((64, 8 * wide), BF),
-        input_output_aliases={4: 0} if out else {},
-        name=name,
-        cost_estimate=pl.CostEstimate(
-            flops=len(chips) * 2 * 64 * 128 * wide,
-            bytes_accessed=len(chips) * wide * 400,
-            transcendentals=0,
-        ),
-        compiler_params=pltpu.CompilerParams(vmem_limit_bytes=32 * 2**20),
-    )(place, offsets, own, got, *out)
+            num_scalar_prefetch=1,
+            grid=(1,),
+            in_specs=whole,
+            out_specs=pl.BlockSpec((64, columns), lambda i, p: (0, 0)),
+        ),
+        out_shape=jax.ShapeDtypeStruct((64, columns), BF),
+        name="finish",
+        compiler_params=pltpu.CompilerParams(vmem_limit_bytes=60 * 2**20),
+    )(place, *own, *got)
 
 
 def per_device(
@@ -429,7 +421,7 @@
         place, q_own, q_got, suffixes, kvs, state, samples, last, name
     )
     state = run([kv[None], kv_core[None]], None, (0, 1), False, "attend_near")
-    ys, state, w_z = hold((ys, state, w_z))
+    ys[0], state, w_z = hold((ys[0], state, w_z))
     w_pair = jnp.concatenate([w, w_z], axis=0)
     w_up, w_down = over_sample(w_pair, YUP), over_sample(w_pair, YDOWN)
     rest = [jnp.concatenate([kv_z[None]] + ys, axis=0)]
@@ -456,9 +448,8 @@
     early = finish_early(from_z)
     late = gather(own, 0, [], arrived, "sum_late")
 
-    out = finish(place, early, over_sample(early, CORE), EARLY_FROM, [], "finish_early")
-    out = finish(place, late, over_sample(late, CORE), LATE_FROM, [out], "finish_late")
-    return out[None]
+    got = [over_sample(early, CORE), over_sample(late, CORE)]
+    return finish(place, [early, late], got)[None]
 
 
 def solution(mesh):

time: 125 us -> 126 us (level)
  the two profiles are of different devices: /device:TPU:97 before, /device:TPU:1 now
where the time goes in v1:
time: 126 us; the launch traced here: 127 us
  Pallas kernels  53.9 us (43%)
  starting transfers between devices  40.3 us (32%)
  waiting for transfers between devices  22.5 us (18%)
  local copies, waits for them, and re-layouts  8.24 us (7%)
  other arithmetic  1.95 us (2%)
    pallas_call x4, Pallas kernels, attend(): pl.pallas_call(functools.partial(attend_kernel, counts, samples, first, l...  28 us
    ppermute x18, starting transfers between devices, over_sample(): return lax.ppermute(value, 'sample', pairs)  22.3 us
    pallas_call x9, Pallas kernels, project(): pl.pallas_call(functools.partial(project_kernel, tiles, len(blocks), [a[2...  21.6 us
    ppermute x11, starting transfers between devices, over_head(): return lax.ppermute(value, 'head', pairs)  18 us
    ppermute x11, waiting for transfers between devices, over_head(): return lax.ppermute(value, 'head', pairs)  17.5 us
    unnamed x22, local copies, waits for them, and re-layouts  5.26 us
    ppermute x18, waiting for transfers between devices, over_sample(): return lax.ppermute(value, 'sample', pairs)  4.98 us
    pallas_call x1, Pallas kernels, finish(): pl.pallas_call(finish_kernel, grid_spec=pltpu.PrefetchScalarGridSpec(num_...  3.38 us
  transfers between devices with their start and end apart: 29, of which 9 were waited for; matrix products, arithmetic and copies ran while one was open for 5% of the time, Pallas kernels for 39%

profile of v1, /device:TPU:1, one launch (start us, length us, event | category | flops | bytes accessed | tf_op | source)
XLA Modules:
  0.0 127.2 jit_solution(17520714509493833498)
XLA Ops:
  3.3 1.7 %collective-permute-start = (bf16[256,256]{1,0:T(8,128)(2,1)S(1)}, bf16[256,256]{1,0:T(8,128)(2,1)}, u32[]{:S(2)}, u32[]{:S(2)}) collective-permute-start(bf16[256,256]{1,0:T(8,128)(2,1)S(1)} %constant_dynamic-update-slice_fusion), channel_id=1, source_target_pairs={{0,64},{8,72},{16,80},{24,88},{32,96},{40,104},{48,112},{56,120},{... | collective-permute-start | bytes 393224 | tf_op jit(solution)/shard_map/ppermute | solution.py:49
  12.1 1.5 %collective-permute-start.7 = (bf16[2,256,256]{2,1,0:T(8,128)(2,1)S(1)}, bf16[2,256,256]{2,1,0:T(8,128)(2,1)S(1)}, u32[]{:S(2)}, u32[]{:S(2)}) collective-permute-start(bf16[2,256,256]{2,1,0:T(8,128)(2,1)S(1)} %pad_maximum_fusion.1), channel_id=1, source_target_pairs={{0,48},{8,56},{16,0},{24,8},{32,16},{40,24},{48,32},{56,40},{64,11... | collective-permute-start | bytes 786440 | tf_op jit(solution)/shard_map/ppermute | solution.py:49
  13.7 1.6 %collective-permute-start.8 = (bf16[2,256,256]{2,1,0:T(8,128)(2,1)S(1)}, bf16[2,256,256]{2,1,0:T(8,128)(2,1)S(1)}, u32[]{:S(2)}, u32[]{:S(2)}) collective-permute-start(bf16[2,256,256]{2,1,0:T(8,128)(2,1)S(1)} %pad_maximum_fusion.1), channel_id=1, source_target_pairs={{0,32},{8,40},{16,48},{24,56},{32,0},{40,8},{48,16},{56,24},{64,96... | collective-permute-start | bytes 786440 | tf_op jit(solution)/shard_map/ppermute | solution.py:49
  17.0 6.3 %attend_near.1 = (f32[2,512,512]{2,1,0:T(8,128)S(1)}, f32[2,512,128]{2,1,0:T(8,128)S(1)}) custom-call(s32[7]{0:T(128)S(1)} %stack.32.place_ref, bf16[512,1024]{1,0:T(8,128)(2,1)S(1)} %bitcast.108, bf16[512,1024]{1,0:T(8,128)(2,1)S(1)} %collective-permute-done.2.q_got_ref, bf16[512,128]{1,0:T(8,128)(2,1)S(1)} %bitcast.113, bf16[512,128]{1,0:T(8,128)(2,1)S(1)} %bitcast.115, ...), custom_call_target="tpu_custom_call" | custom-call | flops 12884901888 | bytes 8388608 | tf_op jit(solution)/shard_map/attend_near/pallas_call | solution.py:188
  23.4 1.6 %collective-permute-done.6 = bf16[320,1024]{1,0:T(8,128)(2,1)S(1)} collective-permute-done((bf16[320,1024]{1,0:T(8,128)(2,1)}, bf16[320,1024]{1,0:T(8,128)(2,1)S(1)}, u32[]{:S(2)}, u32[]{:S(2)}) %collective-permute-start.6) | collective-permute-done | bytes 655392 | tf_op jit(solution)/shard_map/ppermute | solution.py:49
  26.3 1.5 %collective-permute-start.11 = (bf16[640,1024]{1,0:T(8,128)(2,1)S(1)}, bf16[640,1024]{1,0:T(8,128)(2,1)S(1)}, u32[]{:S(2)}, u32[]{:S(2)}) collective-permute-start(bf16[640,1024]{1,0:T(8,128)(2,1)S(1)} %constant_dynamic-update-slice_fusion.2.refs_0_.refs_1_.refs_2_.refs_3_), channel_id=1, source_target_pairs={{0,48},{8,56},{16,0},{24,8},{32,16},{40,24},{48,32},{56,40},{64,11... | collective-permute-start | bytes 3932168 | tf_op jit(solution)/shard_map/ppermute | solution.py:49
  28.9 2.1 %collective-permute-start.9 = (bf16[7,256,256]{2,1,0:T(8,128)(2,1)S(1)}, bf16[7,256,256]{2,1,0:T(8,128)(2,1)S(1)}, u32[]{:S(2)}, u32[]{:S(2)}) collective-permute-start(bf16[7,256,256]{2,1,0:T(8,128)(2,1)S(1)} %pad_maximum_fusion.refs_0_), channel_id=1, source_target_pairs={{0,8},{8,0},{16,24},{24,16},{32,40},{40,32},{48,56},{56,48},{64,72... | collective-permute-start | bytes 2752520 | tf_op jit(solution)/shard_map/ppermute | solution.py:49
  31.0 11.2 %attend_far.1 = (f32[2,512,512]{2,1,0:T(8,128)S(1)}, f32[2,512,128]{2,1,0:T(8,128)S(1)}) custom-call(s32[7]{0:T(128)S(1)} %stack.32.place_ref, bf16[512,1024]{1,0:T(8,128)(2,1)S(1)} %bitcast.109, bf16[512,1024]{1,0:T(8,128)(2,1)S(1)} %collective-permute-done.2.q_got_ref, bf16[7,256,256]{2,1,0:T(8,128)(2,1)S(1)} %pad_maximum_fusion.refs_0_, ...), custom_call_target="tpu_custom_call" | custom-call | flops 30064771072 | bytes 8388608 | tf_op jit(solution)/shard_map/attend_far/pallas_call | solution.py:188
  42.2 6.7 %attend_own.1 = bf16[1,512,512]{2,1,0:T(8,128)(2,1)S(1)} custom-call(s32[7]{0:T(128)S(1)} %stack.32.place_ref, bf16[512,1024]{1,0:T(8,128)(2,1)S(1)} %bitcast.110, bf16[512,1024]{1,0:T(8,128)(2,1)S(1)} %collective-permute-done.2.q_got_ref, bf16[7,256,256]{2,1,0:T(8,128)(2,1)S(1)} %collective-permute-done.9.refs_0_, ...), custom_call_target="tpu_custom_call" | custom-call | flops 15032385536 | bytes 4194304 | tf_op jit(solution)/shard_map/attend_own/pallas_call | solution.py:188
  48.9 3.8 %attend_partner.1 = bf16[1,512,512]{2,1,0:T(8,128)(2,1)S(1)} custom-call(s32[7]{0:T(128)S(1)} %stack.32.place_ref, bf16[512,1024]{1,0:T(8,128)(2,1)S(1)} %bitcast.111, bf16[512,1024]{1,0:T(8,128)(2,1)S(1)} %collective-permute-done.2.q_got_ref, bf16[7,256,256]{2,1,0:T(8,128)(2,1)S(1)} %collective-permute-done.9.refs_0_, ...), custom_call_target="tpu_custom_call" | custom-call | flops 15032385536 | bytes 4194304 | tf_op jit(solution)/shard_map/attend_partner/pallas_call | solution.py:188
  56.4 4.7 %collective-permute-start.17 = (bf16[320,1024]{1,0:T(8,128)(2,1)S(1)}, bf16[320,1024]{1,0:T(8,128)(2,1)S(1)}, u32[]{:S(2)}, u32[]{:S(2)}) collective-permute-start(bf16[320,1024]{1,0:T(8,128)(2,1)S(1)} %slice.7), channel_id=1, source_target_pairs={{0,48},{8,56},{16,0},{24,8},{32,16},{40,24},{48,32},{56,40},{64,11... | collective-permute-start | bytes 1966088 | tf_op jit(solution)/shard_map/ppermute | solution.py:49
  61.0 2.2 %far_low_early.1 = bf16[960,256]{1,0:T(8,128)(2,1)S(1)} custom-call(s32[7]{0:T(128)S(1)} %stack.32.place_ref, bf16[640,1024]{1,0:T(8,128)(2,1)S(1)} %collective-permute-done.10.refs_4_.refs_5_.refs_6_.refs_7_.refs_0_.refs_1_, bf16[640,1024]{1,0:T(8,128)(2,1)S(1)} %collective-permute-done.10.refs_4_.refs_5_.refs_6_.refs_7_.refs_0_.refs_1_, ...), custom_call_target="tpu_custom_call" | custom-call | flops 503316480 | bytes 2457600 | tf_op jit(solution)/shard_map/far_low_early/pallas_call | solution.py:273
  63.2 2.2 %far_top_early.1 = bf16[960,256]{1,0:T(8,128)(2,1)S(1)} custom-call(s32[7]{0:T(128)S(1)} %stack.32.place_ref, bf16[640,1024]{1,0:T(8,128)(2,1)S(1)} %constant_dynamic-update-slice_fusion.2.refs_0_.refs_1_.refs_2_.refs_3_, bf16[640,1024]{1,0:T(8,128)(2,1)S(1)} %constant_dynamic-update-slice_fusion.2.refs_0_.refs_1_.refs_2_.refs_3_, ...), custom_call_target="tpu_custom_call" | custom-call | flops 503316480 | bytes 2457600 | tf_op jit(solution)/shard_map/far_top_early/pallas_call | solution.py:273
  65.5 2.8 %collective-permute-start.15 = (bf16[960,256]{1,0:T(8,128)(2,1)S(1)}, bf16[960,256]{1,0:T(8,128)(2,1)S(1)}, u32[]{:S(2)}, u32[]{:S(2)}) collective-permute-start(bf16[960,256]{1,0:T(8,128)(2,1)S(1)} %far_low_early.1), channel_id=1, source_target_pairs={{0,6},{1,7},{2,0},{3,1},{4,2},{5,3},{6,4},{7,5},{8,14},{9,15},{10,... | collective-permute-start | bytes 1474568 | tf_op jit(solution)/shard_map/ppermute | solution.py:53
  68.2 2.2 %down_top_early.1 = bf16[960,256]{1,0:T(8,128)(2,1)S(1)} custom-call(s32[7]{0:T(128)S(1)} %stack.32.place_ref, bf16[640,1024]{1,0:T(8,128)(2,1)S(1)} %constant_dynamic-update-slice_fusion.2.refs_0_.refs_1_.refs_2_.refs_3_, bf16[640,1024]{1,0:T(8,128)(2,1)S(1)} %constant_dynamic-update-slice_fusion.2.refs_0_.refs_1_.refs_2_.refs_3_, ...), custom_call_target="tpu_custom_call" | custom-call | flops 503316480 | bytes 2457600 | tf_op jit(solution)/shard_map/down_top_early/pallas_call | solution.py:273
  70.5 2.7 %collective-permute-start.20 = (bf16[960,256]{1,0:T(8,128)(2,1)S(1)}, bf16[960,256]{1,0:T(8,128)(2,1)S(1)}, u32[]{:S(2)}, u32[]{:S(2)}) collective-permute-start(bf16[960,256]{1,0:T(8,128)(2,1)S(1)} %down_top_early.1), channel_id=1, source_target_pairs={{0,6},{1,7},{2,0},{3,1},{4,2},{5,3},{6,4},{7,5},{8,14},{9,15},{10,... | collective-permute-start | bytes 1474568 | tf_op jit(solution)/shard_map/ppermute | solution.py:53
  73.2 2.2 %up_low_early.1 = bf16[960,256]{1,0:T(8,128)(2,1)S(1)} custom-call(s32[7]{0:T(128)S(1)} %stack.32.place_ref, bf16[640,1024]{1,0:T(8,128)(2,1)S(1)} %collective-permute-done.10.refs_4_.refs_5_.refs_6_.refs_7_.refs_0_.refs_1_, bf16[640,1024]{1,0:T(8,128)(2,1)S(1)} %collective-permute-done.10.refs_4_.refs_5_.refs_6_.refs_7_.refs_0_.refs_1_, ...), custom_call_target="tpu_custom_call" | custom-call | flops 503316480 | bytes 2457600 | tf_op jit(solution)/shard_map/up_low_early/pallas_call | solution.py:273
  77.1 2.1 %give_late.1 = bf16[640,512]{1,0:T(8,128)(2,1)S(1)} custom-call(s32[7]{0:T(128)S(1)} %stack.32.place_ref, bf16[320,1024]{1,0:T(8,128)(2,1)S(1)} %collective-permute-done.16.refs_0_.refs_1_, bf16[320,1024]{1,0:T(8,128)(2,1)S(1)} %collective-permute-done.16.refs_0_.refs_1_, bf16[320,1024]{1,0:T(8,128)(2,1)S(1)} %collective-permute-done.17.refs_2_.refs_3_, ...), custom_call_target="tpu_custom_call" | custom-call | flops 671088640 | bytes 1966080 | tf_op jit(solution)/shard_map/give_late/pallas_call | solution.py:273
  79.2 2.3 %collective-permute-done.14.refs_14_ = bf16[960,256]{1,0:T(8,128)(2,1)S(1)} collective-permute-done((bf16[960,256]{1,0:T(8,128)(2,1)S(1)}, bf16[960,256]{1,0:T(8,128)(2,1)S(1)}, u32[]{:S(2)}, u32[]{:S(2)}) %collective-permute-start.14) | collective-permute-done | bytes 491552 | tf_op jit(solution)/shard_map/ppermute | solution.py:53
  81.5 2.2 %down_low_early.1 = bf16[960,256]{1,0:T(8,128)(2,1)S(1)} custom-call(s32[7]{0:T(128)S(1)} %stack.32.place_ref, bf16[640,1024]{1,0:T(8,128)(2,1)S(1)} %collective-permute-done.10.refs_4_.refs_5_.refs_6_.refs_7_.refs_0_.refs_1_, bf16[640,1024]{1,0:T(8,128)(2,1)S(1)} %collective-permute-done.10.refs_4_.refs_5_.refs_6_.refs_7_.refs_0_.refs_1_, ...), custom_call_target="tpu_custom_call" | custom-call | flops 503316480 | bytes 2457600 | tf_op jit(solution)/shard_map/down_low_early/pallas_call | solution.py:273
  84.2 2.2 %up_top_early.1 = bf16[960,256]{1,0:T(8,128)(2,1)S(1)} custom-call(s32[7]{0:T(128)S(1)} %stack.32.place_ref, bf16[640,1024]{1,0:T(8,128)(2,1)S(1)} %constant_dynamic-update-slice_fusion.2.refs_0_.refs_1_.refs_2_.refs_3_, bf16[640,1024]{1,0:T(8,128)(2,1)S(1)} %constant_dynamic-update-slice_fusion.2.refs_0_.refs_1_.refs_2_.refs_3_, ...), custom_call_target="tpu_custom_call" | custom-call | flops 503316480 | bytes 2457600 | tf_op jit(solution)/shard_map/up_top_early/pallas_call | solution.py:273
  87.6 3.4 %collective-permute-start.23 = (bf16[640,512]{1,0:T(8,128)(2,1)S(1)}, bf16[640,512]{1,0:T(8,128)(2,1)S(1)}, u32[]{:S(2)}, u32[]{:S(2)}) collective-permute-start(bf16[640,512]{1,0:T(8,128)(2,1)S(1)} %give_late.1), channel_id=1, source_target_pairs={{0,1},{1,0},{2,3},{3,2},{4,5},{5,4},{6,7},{7,6},{8,9},{9,8},{10,11... | collective-permute-start | bytes 1966088 | tf_op jit(solution)/shard_map/ppermute | solution.py:53
  91.0 4.2 %own_early.1.base_ref = f32[1920,256]{1,0:T(8,128)S(1)} custom-call(s32[7]{0:T(128)S(1)} %stack.32.place_ref, bf16[640,1024]{1,0:T(8,128)(2,1)S(1)} %constant_dynamic-update-slice_fusion.2.refs_0_.refs_1_.refs_2_.refs_3_, bf16[640,1024]{1,0:T(8,128)(2,1)S(1)} %constant_dynamic-update-slice_fusion.2.refs_0_.refs_1_.refs_2_.refs_3_, ...), custom_call_target="tpu_custom_call" | custom-call | flops 1006632960 | bytes 4915200 | tf_op jit(solution)/shard_map/own_early/pallas_call | solution.py:273
  95.2 4.3 %collective-permute-done.21.refs_3_ = bf16[960,256]{1,0:T(8,128)(2,1)S(1)} collective-permute-done((bf16[960,256]{1,0:T(8,128)(2,1)S(1)}, bf16[960,256]{1,0:T(8,128)(2,1)S(1)}, u32[]{:S(2)}, u32[]{:S(2)}) %collective-permute-start.21) | collective-permute-done | bytes 491552 | tf_op jit(solution)/shard_map/ppermute | solution.py:53
  99.5 3.1 %collective-permute-done.18.refs_0_ = bf16[960,256]{1,0:T(8,128)(2,1)S(1)} collective-permute-done((bf16[960,256]{1,0:T(8,128)(2,1)S(1)}, bf16[960,256]{1,0:T(8,128)(2,1)S(1)}, u32[]{:S(2)}, u32[]{:S(2)}) %collective-permute-start.18) | collective-permute-done | bytes 491552 | tf_op jit(solution)/shard_map/ppermute | solution.py:53
  103.0 3.5 %collective-permute-start.22 = (bf16[1920,128]{1,0:T(8,128)(2,1)S(1)}, bf16[1920,128]{1,0:T(8,128)(2,1)S(1)}, u32[]{:S(2)}, u32[]{:S(2)}) collective-permute-start(bf16[1920,128]{1,0:T(8,128)(2,1)S(1)} %give_early.1), channel_id=1, source_target_pairs={{0,1},{1,0},{2,3},{3,2},{4,5},{5,4},{6,7},{7,6},{8,9},{9,8},{10,11... | collective-permute-start | bytes 1474568 | tf_op jit(solution)/shard_map/ppermute | solution.py:53
  106.5 2.1 %steps_late.1 = (f32[640,128]{1,0:T(8,128)S(1)}, bf16[640,128]{1,0:T(8,128)(2,1)S(1)}, bf16[640,128]{1,0:T(8,128)(2,1)S(1)}, bf16[640,128]{1,0:T(8,128)(2,1)S(1)}) custom-call(s32[7]{0:T(128)S(1)} %stack.32.place_ref, bf16[320,1024]{1,0:T(8,128)(2,1)S(1)} %collective-permute-done.16.refs_0_.refs_1_, ...), custom_call_target="tpu_custom_call" | custom-call | flops 671088640 | bytes 1966080 | tf_op jit(solution)/shard_map/steps_late/pallas_call | solution.py:273
  109.5 1.9 %collective-permute-start.26 = (bf16[640,128]{1,0:T(8,128)(2,1)S(1)}, bf16[640,128]{1,0:T(8,128)(2,1)S(1)}, u32[]{:S(2)}, u32[]{:S(2)}) collective-permute-start(bf16[640,128]{1,0:T(8,128)(2,1)S(1)} %get-tuple-element.53), channel_id=1, source_target_pairs={{0,6},{1,7},{2,0},{3,1},{4,2},{5,3},{6,4},{7,5},{8,14},{9,15},{10,... | collective-permute-start | bytes 491528 | tf_op jit(solution)/shard_map/ppermute | solution.py:53
  111.4 3.3 %collective-permute-done.24.refs_0_ = bf16[640,128]{1,0:T(8,128)(2,1)S(1)} collective-permute-done((bf16[640,128]{1,0:T(8,128)(2,1)S(1)}, bf16[640,128]{1,0:T(8,128)(2,1)S(1)}, u32[]{:S(2)}, u32[]{:S(2)}) %collective-permute-start.24) | collective-permute-done | bytes 163872 | tf_op jit(solution)/shard_map/ppermute | solution.py:53
  114.7 4.5 %collective-permute-done.25.refs_1_ = bf16[640,128]{1,0:T(8,128)(2,1)S(1)} collective-permute-done((bf16[640,128]{1,0:T(8,128)(2,1)S(1)}, bf16[640,128]{1,0:T(8,128)(2,1)S(1)}, u32[]{:S(2)}, u32[]{:S(2)}) %collective-permute-start.25) | collective-permute-done | bytes 163872 | tf_op jit(solution)/shard_map/ppermute | solution.py:53
  120.9 1.5 %collective-permute-done.28.got_late_ref = bf16[640,128]{1,0:T(8,128)(2,1)S(1)} collective-permute-done((bf16[640,128]{1,0:T(8,128)(2,1)S(1)}, bf16[640,128]{1,0:T(8,128)(2,1)S(1)}, u32[]{:S(2)}, u32[]{:S(2)}) %collective-permute-start.28) | collective-permute-done | bytes 163872 | tf_op jit(solution)/shard_map/ppermute | solution.py:49
  123.9 3.4 %finish.1 = bf16[64,5120]{1,0:T(8,128)(2,1)} custom-call(s32[7]{0:T(128)} %copy-done.2, bf16[1920,128]{1,0:T(8,128)(2,1)} %copy-done, bf16[640,128]{1,0:T(8,128)(2,1)} %copy-done.1, bf16[1920,128]{1,0:T(8,128)(2,1)} %copy-done.7, bf16[640,128]{1,0:T(8,128)(2,1)} %copy-done.8), custom_call_target="tpu_custom_call" | custom-call | tf_op jit(solution)/shard_map/finish/pallas_call | solution.py:381
  (73 shorter events, 26.1 us)
Async XLA Ops:
  0.0 15.2 %copy-start.3 = (bf16[1,512,1024]{2,1,0:T(8,128)(2,1)S(1)}, bf16[1,512,1024]{2,1,0:T(8,128)(2,1)}, u32[]{:S(2)}) copy-start(bf16[1,512,1024]{2,1,0:T(8,128)(2,1)} %param.7) | copy-start | bytes 3145732
  0.0 6.9 %copy-start.9 = (s32[16]{0:T(128)S(1)}, s32[16]{0:T(128)}, u32[]{:S(2)}) copy-start(s32[16]{0:T(128)} %param.12) | copy-start | bytes 196
  0.0 15.2 %collective-permute-start.2 = (bf16[512,1024]{1,0:T(8,128)(2,1)}, bf16[512,1024]{1,0:T(8,128)(2,1)S(1)}, u32[]{:S(2)}, u32[]{:S(2)}) collective-permute-start(bf16[512,1024]{1,0:T(8,128)(2,1)} %bitcast.107), channel_id=1, source_target_pairs={{0,8},{8,0},{16,24},{24,16},{32,40},{40,32},{48,56},{56,48},{64,72... | collective-permute-start | bytes 3145736 | tf_op jit(solution)/shard_map/ppermute | solution.py:49
  3.1 7.6 %collective-permute-start.5 = (bf16[256,256]{1,0:T(8,128)(2,1)S(1)}, bf16[256,256]{1,0:T(8,128)(2,1)}, u32[]{:S(2)}, u32[]{:S(2)}) collective-permute-start(bf16[256,256]{1,0:T(8,128)(2,1)S(1)} %constant_dynamic-update-slice_fusion), channel_id=1, source_target_pairs={{0,8},{8,0},{16,24},{24,16},{32,40},{40,32},{48,56},{56,48},{64,72... | collective-permute-start | bytes 393224 | tf_op jit(solution)/shard_map/ppermute | solution.py:49
  3.3 5.6 %collective-permute-start = (bf16[256,256]{1,0:T(8,128)(2,1)S(1)}, bf16[256,256]{1,0:T(8,128)(2,1)}, u32[]{:S(2)}, u32[]{:S(2)}) collective-permute-start(bf16[256,256]{1,0:T(8,128)(2,1)S(1)} %constant_dynamic-update-slice_fusion), channel_id=1, source_target_pairs={{0,64},{8,72},{16,80},{24,88},{32,96},{40,104},{48,112},{56,120},{... | collective-permute-start | bytes 393224 | tf_op jit(solution)/shard_map/ppermute | solution.py:49
  5.0 7.1 %collective-permute-start.3 = (bf16[512,128]{1,0:T(8,128)(2,1)}, bf16[512,128]{1,0:T(8,128)(2,1)}, u32[]{:S(2)}, u32[]{:S(2)}) collective-permute-start(bf16[512,128]{1,0:T(8,128)(2,1)} %bitcast.112), channel_id=1, source_target_pairs={{0,8},{8,0},{16,24},{24,16},{32,40},{40,32},{48,56},{56,48},{64,72... | collective-permute-start | bytes 393224 | tf_op jit(solution)/shard_map/ppermute | solution.py:49
  5.7 7.9 %collective-permute-start.4 = (bf16[512,128]{1,0:T(8,128)(2,1)}, bf16[512,128]{1,0:T(8,128)(2,1)}, u32[]{:S(2)}, u32[]{:S(2)}) collective-permute-start(bf16[512,128]{1,0:T(8,128)(2,1)} %bitcast.114), channel_id=1, source_target_pairs={{0,8},{8,0},{16,24},{24,16},{32,40},{40,32},{48,56},{56,48},{64,72... | collective-permute-start | bytes 393224 | tf_op jit(solution)/shard_map/ppermute | solution.py:49
  8.9 97.5 %copy-start.2 = (s32[7]{0:T(128)}, s32[7]{0:T(128)S(1)}, u32[]{:S(2)}) copy-start(s32[7]{0:T(128)S(1)} %stack.32.place_ref) | copy-start | bytes 88
  8.9 16.0 %collective-permute-start.6 = (bf16[320,1024]{1,0:T(8,128)(2,1)}, bf16[320,1024]{1,0:T(8,128)(2,1)S(1)}, u32[]{:S(2)}, u32[]{:S(2)}) collective-permute-start(bf16[320,1024]{1,0:T(8,128)(2,1)} %bitcast.117), channel_id=1, source_target_pairs={{0,64},{8,72},{16,80},{24,88},{32,96},{40,104},{48,112},{56,120},{... | collective-permute-start | bytes 1966088 | tf_op jit(solution)/shard_map/ppermute | solution.py:49
  10.8 12.6 %collective-permute-start.1 = (bf16[2,256,256]{2,1,0:T(8,128)(2,1)S(1)}, bf16[2,256,256]{2,1,0:T(8,128)(2,1)S(1)}, u32[]{:S(2)}, u32[]{:S(2)}) collective-permute-start(bf16[2,256,256]{2,1,0:T(8,128)(2,1)S(1)} %pad_maximum_fusion.1), channel_id=1, source_target_pairs={{0,16},{8,24},{16,32},{24,40},{32,48},{40,56},{48,0},{56,8},{64,80... | collective-permute-start | bytes 786440 | tf_op jit(solution)/shard_map/ppermute | solution.py:49
  12.1 15.7 %collective-permute-start.7 = (bf16[2,256,256]{2,1,0:T(8,128)(2,1)S(1)}, bf16[2,256,256]{2,1,0:T(8,128)(2,1)S(1)}, u32[]{:S(2)}, u32[]{:S(2)}) collective-permute-start(bf16[2,256,256]{2,1,0:T(8,128)(2,1)S(1)} %pad_maximum_fusion.1), channel_id=1, source_target_pairs={{0,48},{8,56},{16,0},{24,8},{32,16},{40,24},{48,32},{56,40},{64,11... | collective-permute-start | bytes 786440 | tf_op jit(solution)/shard_map/ppermute | solution.py:49
  13.7 14.2 %collective-permute-start.8 = (bf16[2,256,256]{2,1,0:T(8,128)(2,1)S(1)}, bf16[2,256,256]{2,1,0:T(8,128)(2,1)S(1)}, u32[]{:S(2)}, u32[]{:S(2)}) collective-permute-start(bf16[2,256,256]{2,1,0:T(8,128)(2,1)S(1)} %pad_maximum_fusion.1), channel_id=1, source_target_pairs={{0,32},{8,40},{16,48},{24,56},{32,0},{40,8},{48,16},{56,24},{64,96... | collective-permute-start | bytes 786440 | tf_op jit(solution)/shard_map/ppermute | solution.py:49
  25.0 30.2 %collective-permute-start.10 = (bf16[640,1024]{1,0:T(8,128)(2,1)S(1)}, bf16[640,1024]{1,0:T(8,128)(2,1)S(1)}, u32[]{:S(2)}, u32[]{:S(2)}) collective-permute-start(bf16[640,1024]{1,0:T(8,128)(2,1)S(1)} %constant_dynamic-update-slice_fusion.2.refs_0_.refs_1_.refs_2_.refs_3_), channel_id=1, source_target_pairs={{0,16},{8,24},{16,32},{24,40},{32,48},{40,56},{48,0},{56,8},{64,80... | collective-permute-start | bytes 3932168 | tf_op jit(solution)/shard_map/ppermute | solution.py:49
  26.3 28.9 %collective-permute-start.11 = (bf16[640,1024]{1,0:T(8,128)(2,1)S(1)}, bf16[640,1024]{1,0:T(8,128)(2,1)S(1)}, u32[]{:S(2)}, u32[]{:S(2)}) collective-permute-start(bf16[640,1024]{1,0:T(8,128)(2,1)S(1)} %constant_dynamic-update-slice_fusion.2.refs_0_.refs_1_.refs_2_.refs_3_), channel_id=1, source_target_pairs={{0,48},{8,56},{16,0},{24,8},{32,16},{40,24},{48,32},{56,40},{64,11... | collective-permute-start | bytes 3932168 | tf_op jit(solution)/shard_map/ppermute | solution.py:49
  28.9 13.3 %collective-permute-start.9 = (bf16[7,256,256]{2,1,0:T(8,128)(2,1)S(1)}, bf16[7,256,256]{2,1,0:T(8,128)(2,1)S(1)}, u32[]{:S(2)}, u32[]{:S(2)}) collective-permute-start(bf16[7,256,256]{2,1,0:T(8,128)(2,1)S(1)} %pad_maximum_fusion.refs_0_), channel_id=1, source_target_pairs={{0,8},{8,0},{16,24},{24,16},{32,40},{40,32},{48,56},{56,48},{64,72... | collective-permute-start | bytes 2752520 | tf_op jit(solution)/shard_map/ppermute | solution.py:49
  52.7 8.3 %collective-permute-start.12 = (bf16[1,512,512]{2,1,0:T(8,128)(2,1)S(1)}, bf16[1,512,512]{2,1,0:T(8,128)(2,1)S(1)}, u32[]{:S(2)}, u32[]{:S(2)}) collective-permute-start(bf16[1,512,512]{2,1,0:T(8,128)(2,1)S(1)} %attend_partner.1), channel_id=1, source_target_pairs={{0,8},{8,0},{16,24},{24,16},{32,40},{40,32},{48,56},{56,48},{64,72... | collective-permute-start | bytes 1572872 | tf_op jit(solution)/shard_map/ppermute | solution.py:49
  53.8 7.3 %collective-permute-start.13 = (bf16[1,512,512]{2,1,0:T(8,128)(2,1)S(1)}, bf16[1,512,512]{2,1,0:T(8,128)(2,1)S(1)}, u32[]{:S(2)}, u32[]{:S(2)}) collective-permute-start(bf16[1,512,512]{2,1,0:T(8,128)(2,1)S(1)} %attend_own.1), channel_id=1, source_target_pairs={{0,8},{8,0},{16,24},{24,16},{32,40},{40,32},{48,56},{56,48},{64,72... | collective-permute-start | bytes 1572872 | tf_op jit(solution)/shard_map/ppermute | solution.py:49
  55.3 20.6 %collective-permute-start.16 = (bf16[320,1024]{1,0:T(8,128)(2,1)S(1)}, bf16[320,1024]{1,0:T(8,128)(2,1)S(1)}, u32[]{:S(2)}, u32[]{:S(2)}) collective-permute-start(bf16[320,1024]{1,0:T(8,128)(2,1)S(1)} %slice.6), channel_id=1, source_target_pairs={{0,16},{8,24},{16,32},{24,40},{32,48},{40,56},{48,0},{56,8},{64,80... | collective-permute-start | bytes 1966088 | tf_op jit(solution)/shard_map/ppermute | solution.py:49
  56.4 20.8 %collective-permute-start.17 = (bf16[320,1024]{1,0:T(8,128)(2,1)S(1)}, bf16[320,1024]{1,0:T(8,128)(2,1)S(1)}, u32[]{:S(2)}, u32[]{:S(2)}) collective-permute-start(bf16[320,1024]{1,0:T(8,128)(2,1)S(1)} %slice.7), channel_id=1, source_target_pairs={{0,48},{8,56},{16,0},{24,8},{32,16},{40,24},{48,32},{56,40},{64,11... | collective-permute-start | bytes 1966088 | tf_op jit(solution)/shard_map/ppermute | solution.py:49
  65.5 13.7 %collective-permute-start.15 = (bf16[960,256]{1,0:T(8,128)(2,1)S(1)}, bf16[960,256]{1,0:T(8,128)(2,1)S(1)}, u32[]{:S(2)}, u32[]{:S(2)}) collective-permute-start(bf16[960,256]{1,0:T(8,128)(2,1)S(1)} %far_low_early.1), channel_id=1, source_target_pairs={{0,6},{1,7},{2,0},{3,1},{4,2},{5,3},{6,4},{7,5},{8,14},{9,15},{10,... | collective-permute-start | bytes 1474568 | tf_op jit(solution)/shard_map/ppermute | solution.py:53
  68.2 13.3 %collective-permute-start.14 = (bf16[960,256]{1,0:T(8,128)(2,1)S(1)}, bf16[960,256]{1,0:T(8,128)(2,1)S(1)}, u32[]{:S(2)}, u32[]{:S(2)}) collective-permute-start(bf16[960,256]{1,0:T(8,128)(2,1)S(1)} %far_top_early.1), channel_id=1, source_target_pairs={{0,2},{1,3},{2,4},{3,5},{4,6},{5,7},{6,0},{7,1},{8,10},{9,11},{10,... | collective-permute-start | bytes 1474568 | tf_op jit(solution)/shard_map/ppermute | solution.py:53
  70.5 24.7 %collective-permute-start.20 = (bf16[960,256]{1,0:T(8,128)(2,1)S(1)}, bf16[960,256]{1,0:T(8,128)(2,1)S(1)}, u32[]{:S(2)}, u32[]{:S(2)}) collective-permute-start(bf16[960,256]{1,0:T(8,128)(2,1)S(1)} %down_top_early.1), channel_id=1, source_target_pairs={{0,6},{1,7},{2,0},{3,1},{4,2},{5,3},{6,4},{7,5},{8,14},{9,15},{10,... | collective-permute-start | bytes 1474568 | tf_op jit(solution)/shard_map/ppermute | solution.py:53
  75.9 19.3 %collective-permute-start.19 = (bf16[960,256]{1,0:T(8,128)(2,1)S(1)}, bf16[960,256]{1,0:T(8,128)(2,1)S(1)}, u32[]{:S(2)}, u32[]{:S(2)}) collective-permute-start(bf16[960,256]{1,0:T(8,128)(2,1)S(1)} %up_low_early.1), channel_id=1, source_target_pairs={{0,2},{1,3},{2,4},{3,5},{4,6},{5,7},{6,0},{7,1},{8,10},{9,11},{10,... | collective-permute-start | bytes 1474568 | tf_op jit(solution)/shard_map/ppermute | solution.py:53
  83.8 15.7 %collective-permute-start.21 = (bf16[960,256]{1,0:T(8,128)(2,1)S(1)}, bf16[960,256]{1,0:T(8,128)(2,1)S(1)}, u32[]{:S(2)}, u32[]{:S(2)}) collective-permute-start(bf16[960,256]{1,0:T(8,128)(2,1)S(1)} %down_low_early.1), channel_id=1, source_target_pairs={{0,6},{1,7},{2,0},{3,1},{4,2},{5,3},{6,4},{7,5},{8,14},{9,15},{10,... | collective-permute-start | bytes 1474568 | tf_op jit(solution)/shard_map/ppermute | solution.py:53
  86.4 16.2 %collective-permute-start.18 = (bf16[960,256]{1,0:T(8,128)(2,1)S(1)}, bf16[960,256]{1,0:T(8,128)(2,1)S(1)}, u32[]{:S(2)}, u32[]{:S(2)}) collective-permute-start(bf16[960,256]{1,0:T(8,128)(2,1)S(1)} %up_top_early.1), channel_id=1, source_target_pairs={{0,2},{1,3},{2,4},{3,5},{4,6},{5,7},{6,0},{7,1},{8,10},{9,11},{10,... | collective-permute-start | bytes 1474568 | tf_op jit(solution)/shard_map/ppermute | solution.py:53
  87.6 18.9 %collective-permute-start.23 = (bf16[640,512]{1,0:T(8,128)(2,1)S(1)}, bf16[640,512]{1,0:T(8,128)(2,1)S(1)}, u32[]{:S(2)}, u32[]{:S(2)}) collective-permute-start(bf16[640,512]{1,0:T(8,128)(2,1)S(1)} %give_late.1), channel_id=1, source_target_pairs={{0,1},{1,0},{2,3},{3,2},{4,5},{5,4},{6,7},{7,6},{8,9},{9,8},{10,11... | collective-permute-start | bytes 1966088 | tf_op jit(solution)/shard_map/ppermute | solution.py:53
  103.0 16.1 %collective-permute-start.22 = (bf16[1920,128]{1,0:T(8,128)(2,1)S(1)}, bf16[1920,128]{1,0:T(8,128)(2,1)S(1)}, u32[]{:S(2)}, u32[]{:S(2)}) collective-permute-start(bf16[1920,128]{1,0:T(8,128)(2,1)S(1)} %give_early.1), channel_id=1, source_target_pairs={{0,1},{1,0},{2,3},{3,2},{4,5},{5,4},{6,7},{7,6},{8,9},{9,8},{10,11... | collective-permute-start | bytes 1474568 | tf_op jit(solution)/shard_map/ppermute | solution.py:53
  108.6 6.1 %collective-permute-start.24 = (bf16[640,128]{1,0:T(8,128)(2,1)S(1)}, bf16[640,128]{1,0:T(8,128)(2,1)S(1)}, u32[]{:S(2)}, u32[]{:S(2)}) collective-permute-start(bf16[640,128]{1,0:T(8,128)(2,1)S(1)} %get-tuple-element.51), channel_id=1, source_target_pairs={{0,4},{1,5},{2,6},{3,7},{4,0},{5,1},{6,2},{7,3},{8,12},{9,13},{10,... | collective-permute-start | bytes 491528 | tf_op jit(solution)/shard_map/ppermute | solution.py:53
  108.7 10.5 %collective-permute-start.25 = (bf16[640,128]{1,0:T(8,128)(2,1)S(1)}, bf16[640,128]{1,0:T(8,128)(2,1)S(1)}, u32[]{:S(2)}, u32[]{:S(2)}) collective-permute-start(bf16[640,128]{1,0:T(8,128)(2,1)S(1)} %get-tuple-element.52), channel_id=1, source_target_pairs={{0,2},{1,3},{2,4},{3,5},{4,6},{5,7},{6,0},{7,1},{8,10},{9,11},{10,... | collective-permute-start | bytes 491528 | tf_op jit(solution)/shard_map/ppermute | solution.py:53
  109.5 9.6 %collective-permute-start.26 = (bf16[640,128]{1,0:T(8,128)(2,1)S(1)}, bf16[640,128]{1,0:T(8,128)(2,1)S(1)}, u32[]{:S(2)}, u32[]{:S(2)}) collective-permute-start(bf16[640,128]{1,0:T(8,128)(2,1)S(1)} %get-tuple-element.53), channel_id=1, source_target_pairs={{0,6},{1,7},{2,0},{3,1},{4,2},{5,3},{6,4},{7,5},{8,14},{9,15},{10,... | collective-permute-start | bytes 491528 | tf_op jit(solution)/shard_map/ppermute | solution.py:53
  119.7 2.7 %collective-permute-start.27 = (bf16[1920,128]{1,0:T(8,128)(2,1)S(1)}, bf16[1920,128]{1,0:T(8,128)(2,1)S(1)}, u32[]{:S(2)}, u32[]{:S(2)}) collective-permute-start(bf16[1920,128]{1,0:T(8,128)(2,1)S(1)} %sum_early.1.own_early_ref), channel_id=1, source_target_pairs={{0,8},{8,0},{16,24},{24,16},{32,40},{40,32},{48,56},{56,48},{64,72... | collective-permute-start | bytes 1474568 | tf_op jit(solution)/shard_map/ppermute | solution.py:49
  120.8 1.6 %collective-permute-start.28 = (bf16[640,128]{1,0:T(8,128)(2,1)S(1)}, bf16[640,128]{1,0:T(8,128)(2,1)S(1)}, u32[]{:S(2)}, u32[]{:S(2)}) collective-permute-start(bf16[640,128]{1,0:T(8,128)(2,1)S(1)} %sum_late.1.own_late_ref), channel_id=1, source_target_pairs={{0,8},{8,0},{16,24},{24,16},{32,40},{40,32},{48,56},{56,48},{64,72... | collective-permute-start | bytes 491528 | tf_op jit(solution)/shard_map/ppermute | solution.py:49
  (7 other events, 13.2 us)
